TPU v7x, 512 devices: a whole 4x4x16 slice. The times are simulated.
512 devices in a mesh: lev: 16 (over z), lat: 32 (over x, y, core).
Axes of the slice: x: 4, y: 4, z: 16, core: 2. Of those that a mesh axis runs over, the one named last changes fastest.
Arguments:
- adjoint_in: float32 [2, 32, 512, 1024], P(None, 'lev', 'lat'), may hold values from -6 to 6
- courant: float32 [2, 32, 512, 1024], P(None, None, 'lat', 'lev'), may hold values from -0.6 to 0.6
- cloud_top: int32 [512, 1024], P('lat', 'lev'), may hold values from 0 to 15
- conv_inverse: float32 [16, 32, 32], replicated
- sounding_kernel: float32 [16, 32, 512, 64], P('lev', 'lat'), may hold values from -6 to 6
- sounding_weight: float32 [16, 32, 512, 2], P('lev', 'lat'), may hold values from -6 to 6
- sounding_owner: int32 [16, 32, 512], P('lev', 'lat'), may hold values from 0 to 31, as said below
- sounding_cell: int32 [16, 32, 512], P('lev', 'lat'), may hold values from 0 to 1023
- sounding_count: int32 [16, 32], P('lev', 'lat'), may hold values from 384 to 512
Outputs:
- adjoint_out: float32 [2, 32, 512, 1024], P(None, 'lev', 'lat')
- sensitivity: float32 [16, 32, 512, 2], P('lev', 'lat')
Inputs may be any that keep to these rules, and one draw needn't show every extreme that they name: `sounding_owner`: of the sounding slots of one device, at most 48 name any one band.
All inputs are finite; a program needn't handle non-finite values.
Results may differ from a plain program's by a relative error of at most 0.0003.
Values sent between devices are 32-bit elements; how exact they have to be, the bound alone decides.
A program may use at most 64 MiB of HBM per device.

v0:
```python
import math

import jax
import jax.numpy as jnp
from jax import lax
from jax.sharding import PartitionSpec as P


def with_halo(block, sides, width):
    for axis, dim in sides:
        count = lax.axis_size(axis)
        forward = [(i, i + 1) for i in range(count - 1)]
        backward = [(target, source) for source, target in forward]
        low = lax.ppermute(
            lax.slice_in_dim(block, block.shape[dim] - width, None, axis=dim), axis, forward
        )
        high = lax.ppermute(lax.slice_in_dim(block, 0, width, axis=dim), axis, backward)
        block = jnp.concatenate([low, block, high], axis=dim)
    return block


def trim(array, along, start, length):
    return lax.slice_in_dim(array, start, start + length, axis=along % array.ndim)


def face_flux(field, cour, along, extent):
    back_two = trim(field, along, 0, extent + 5)
    back_one = trim(field, along, 1, extent + 5)
    center = trim(field, along, 2, extent + 5)
    ahead = trim(field, along, 3, extent + 5)
    speed = trim(cour, along, 1, extent + 5)
    upwind = speed * (back_one + 0.25 * (1.0 - speed) * (center - back_two))
    downwind = speed * (center - 0.25 * (1.0 + speed) * (ahead - back_one))
    return jnp.where(speed >= 0.0, upwind, downwind)


def forward_step(field, cour_x, cour_y, lat_count, lon_count):
    rows_x = trim(field, -2, 2, lat_count + 4)
    speed_x = trim(cour_x, -2, 1, lat_count + 4)
    flux_x = face_flux(rows_x, speed_x, -1, lon_count)
    div_x = trim(flux_x, -1, 1, lon_count + 4) - trim(flux_x, -1, 0, lon_count + 4)
    cols_y = trim(field, -1, 2, lon_count + 4)
    speed_y = trim(cour_y, -1, 1, lon_count + 4)
    flux_y = face_flux(cols_y, speed_y, -2, lat_count)
    div_y = trim(flux_y, -2, 1, lat_count + 4) - trim(flux_y, -2, 0, lat_count + 4)
    center = trim(trim(field, -2, 2, lat_count + 4), -1, 2, lon_count + 4)
    return center - div_x - div_y


def adjoint_step(adj_inner, cour_x, cour_y, lat_count, lon_count):
    shape_full = adj_inner.shape[:-2] + (lat_count + 8, lon_count + 8)
    start = jnp.zeros(shape_full, adj_inner.dtype)
    _, pullback = jax.vjp(
        lambda field: forward_step(field, cour_x, cour_y, lat_count, lon_count), start
    )
    grad_field = pullback(adj_inner)[0]
    return grad_field[..., 4 : lat_count + 4, 4 : lon_count + 4]


def local_adjoint(padded, global_row, lat_total):
    inside = (global_row >= 0) & (global_row < lat_total)
    keep_row = inside[:, None]
    adj_all = jnp.where(keep_row, padded[0:2], 0.0)
    cour_x = jnp.where(keep_row, padded[2], 0.0)
    cour_y = jnp.where(keep_row & (global_row != 0)[:, None], padded[3], 0.0)
    lat_count = padded.shape[-2] - 6
    lon_count = padded.shape[-1] - 6
    return adjoint_step(adj_all[..., 1:-1, 1:-1], cour_x, cour_y, lat_count, lon_count)


def one_hot_rows(target, columns):
    return (target[:, None] == jnp.arange(columns, dtype=jnp.int32)[None, :]).astype(jnp.float32)


def deposit_rows(target, weighted, columns):
    rows = target.shape[0]
    block = math.gcd(rows, 256)
    blocks = rows // block
    target_blocks = target.reshape(blocks, block)
    weighted_blocks = weighted.reshape((blocks, block) + weighted.shape[1:])

    def add_block(total, pieces):
        hot = one_hot_rows(pieces[0], columns)
        part_sum = jnp.einsum("mc,mtk->tkc", hot, pieces[1], precision=lax.Precision.HIGHEST)
        return (total + part_sum, None)

    start = jnp.zeros((weighted.shape[1], weighted.shape[2], columns), jnp.float32)
    total, _ = lax.scan(add_block, start, (target_blocks, weighted_blocks))
    return total


def sense_rows(target, kernel_rows, adj_conv, columns):
    rows = target.shape[0]
    block = math.gcd(rows, 256)
    blocks = rows // block
    target_blocks = target.reshape(blocks, block)
    kernel_blocks = kernel_rows.reshape((blocks, block) + kernel_rows.shape[1:])

    def one_block(pieces):
        hot = one_hot_rows(pieces[0], columns)
        picked = jnp.einsum("mc,tkc->mtk", hot, adj_conv, precision=lax.Precision.HIGHEST)
        return jnp.sum(pieces[1] * picked, axis=2)

    result = lax.map(one_block, (target_blocks, kernel_blocks))
    return result.reshape(rows, kernel_rows.shape[1])


def per_device(
    adjoint_in,
    courant,
    cloud_top,
    conv_inverse,
    sounding_kernel,
    sounding_weight,
    sounding_owner,
    sounding_cell,
    sounding_count,
):
    bands = lax.axis_size("lat")
    adj_cols = lax.all_to_all(adjoint_in, "lev", split_axis=3, concat_axis=1, tiled=True)
    band_rows = adj_cols.shape[2]
    piece_width = adj_cols.shape[3]
    levels_all = adj_cols.shape[1]
    columns = band_rows * piece_width
    adj_mixed = adj_cols.reshape(2, levels_all, columns)
    slots_held = sounding_kernel.shape[2]
    kernels = sounding_kernel.reshape(slots_held, 2 * levels_all)
    weights = sounding_weight.reshape(slots_held, 2)
    owners = sounding_owner.reshape(slots_held)
    cells = sounding_cell.reshape(slots_held)
    held_count = sounding_count.reshape(())
    is_valid = jnp.arange(slots_held, dtype=jnp.int32) < held_count
    capacity = 3 * slots_held // bands
    slots_all = bands * capacity
    one_hot = (
        (owners[:, None] == jnp.arange(bands, dtype=jnp.int32)[None, :]) & is_valid[:, None]
    ).astype(jnp.float32)
    slot_ids = jnp.arange(slots_held, dtype=jnp.int32)
    strictly_below = (slot_ids[None, :] < slot_ids[:, None]).astype(jnp.float32)
    before = jnp.dot(
        strictly_below, one_hot, precision=lax.Precision.HIGHEST, preferred_element_type=jnp.float32
    )
    rank_in = jnp.sum(before * one_hot, axis=1).astype(jnp.int32)
    slot_of = jnp.where(is_valid, owners * capacity + rank_in, slots_all)
    placing = (jnp.arange(slots_all, dtype=jnp.int32)[:, None] == slot_of[None, :]).astype(
        jnp.float32
    )
    buf_kernels = jnp.dot(
        placing, kernels, precision=lax.Precision.HIGHEST, preferred_element_type=jnp.float32
    )
    buf_weights = jnp.dot(
        placing, weights, precision=lax.Precision.HIGHEST, preferred_element_type=jnp.float32
    )
    buf_place = (
        jnp.dot(
            placing,
            (cells + 1).astype(jnp.float32),
            precision=lax.Precision.HIGHEST,
            preferred_element_type=jnp.float32,
        )
        - 1.0
    )
    got_kernels, got_weights, got_place = (
        lax.all_to_all(buf_kernels, "lat", split_axis=0, concat_axis=0, tiled=True),
        lax.all_to_all(buf_weights, "lat", split_axis=0, concat_axis=0, tiled=True),
        lax.all_to_all(buf_place, "lat", split_axis=0, concat_axis=0, tiled=True),
    )
    local_col = got_place.astype(jnp.int32)
    usable = local_col >= 0
    target = jnp.where(usable, local_col, columns)
    kernel_rows = got_kernels.reshape(-1, 2, levels_all)
    deposit = deposit_rows(target, got_weights[:, :, None] * kernel_rows, columns)
    adj_mixed = adj_mixed + deposit
    tops = cloud_top.reshape(columns)

    def mix_class(top_class, running):
        matrix = lax.dynamic_index_in_dim(conv_inverse, top_class, 0, keepdims=False)
        mixed = jnp.einsum("kj,tkn->tjn", matrix, adj_mixed, precision=lax.Precision.HIGHEST)
        return running + jnp.where(tops[None, None, :] == top_class, mixed, 0.0)

    adj_conv = lax.fori_loop(
        0, conv_inverse.shape[0], mix_class, jnp.zeros((2, levels_all, columns), jnp.float32)
    )
    sens_rows = sense_rows(target, kernel_rows, adj_conv, columns)
    sens_rows = jnp.where(usable[:, None], sens_rows, 0.0)
    returned = lax.all_to_all(sens_rows, "lat", split_axis=0, concat_axis=0, tiled=True)
    own_part = jnp.einsum("as,at->st", placing, returned, precision=lax.Precision.HIGHEST)
    own_part = jnp.where(is_valid[:, None], own_part, 0.0)
    sensitivity = own_part.reshape(1, 1, slots_held, 2)
    adj_grid = adj_conv.reshape(2, levels_all, band_rows, piece_width)
    lat_total = band_rows * bands
    global_row = lax.axis_index("lat") * band_rows - 3 + jnp.arange(band_rows + 6, dtype=jnp.int32)
    adj_slab, cour_slab = (
        lax.all_to_all(adj_grid, "lev", split_axis=1, concat_axis=3, tiled=True),
        lax.all_to_all(courant, "lev", split_axis=1, concat_axis=3, tiled=True),
    )
    stacked = jnp.concatenate([adj_slab, cour_slab], axis=0)
    padded = with_halo(stacked, (("lat", 2),), 3)
    padded = jnp.concatenate([padded[..., -3:], padded, padded[..., :3]], axis=3)
    adjoint_out = local_adjoint(padded, global_row, lat_total)
    return (adjoint_out, sensitivity)


def solution(mesh):
    placed = (
        P(None, "lev", "lat", None),
        P(None, None, "lat", "lev"),
        P("lat", "lev"),
        P(),
        P("lev", "lat", None, None),
        P("lev", "lat", None, None),
        P("lev", "lat", None),
        P("lev", "lat", None),
        P("lev", "lat"),
    )
    return jax.shard_map(
        per_device,
        mesh=mesh,
        in_specs=placed,
        out_specs=(P(None, "lev", "lat", None), P("lev", "lat", None, None)),
        check_vma=False,
    )
```

profile of v0, /device:TPU:1, one launch (start us, length us, event | category | flops | bytes accessed | tf_op | source)
XLA Modules:
  0.0 183.3 jit_solution(11599901403547196440)
XLA Ops:
  3.1 2.2 %fusion.25 = f32[1536]{0:T(1024)S(1)} fusion(s32[512]{0:T(512)S(1)} %add_select_fusion, s32[1,1,512]{2,1,0:T(1,128)} %param.22), kind=kOutput, calls=%fused_computation.37 | convolution fusion | flops 10224640 | bytes 10240 | tf_op jit(solution)/shard_map/dot_general | solution.py:155
  6.0 10.4 %all-to-all-start.3 = ((f32[32,48,1]{1,2,0:T(1,128)}), f32[32,48,1]{1,2,0:T(1,128)S(1)}, u32[]{:S(2)}, u32[]{:S(2)}) async-start(f32[32,48,1]{1,2,0:T(1,128)} %all_to_all.62), calls=%async_computation.3 | async-start | bytes 32768 | tf_op jit(solution)/shard_map/all_to_all | solution.py:166
  16.4 3.7 %fusion.14 = f32[32,48,2]{1,2,0:T(2,128)} fusion(s32[512]{0:T(512)S(1)} %add_select_fusion, s32[32,48]{1,0:T(8,128)S(1)} %multiply_add_fusion.2, f32[1,1,512,2]{2,3,1,0:T(2,128)} %param.20), kind=kOutput, calls=%fused_computation.24 | convolution fusion | flops 19660800 | bytes 24576 | tf_op jit(solution)/shard_map/dot_general | solution.py:151
  20.1 3.2 %all-to-all-done.3 = f32[32,48,1]{1,2,0:T(1,128)S(1)} async-done(((f32[32,48,1]{1,2,0:T(1,128)}), f32[32,48,1]{1,2,0:T(1,128)S(1)}, u32[]{:S(2)}, u32[]{:S(2)}) %all-to-all-start.3) | async-done | bytes 6176 | tf_op jit(solution)/shard_map/all_to_all | solution.py:166
  23.4 4.2 %all-to-all-start.1 = ((f32[32,48,2]{1,2,0:T(2,128)}), f32[32,48,2]{1,2,0:T(2,128)S(1)}, u32[]{:S(2)}, u32[]{:S(2)}) async-start(f32[32,48,2]{1,2,0:T(2,128)} %fusion.14), calls=%async_computation.1 | async-start | bytes 65536 | tf_op jit(solution)/shard_map/all_to_all | solution.py:165
  27.6 1.4 fusion.12
  29.1 1.2 reshape.162
  30.3 1.3 copy.47
  31.7 3.6 %reshape.160 = f32[16,1,4096]{2,1,0:T(1,128)} reshape(f32[1024,2,2,16]{3,2,1,0:T(2,128)S(1)} %bitcast.115) | data formatting | bytes 524288
  37.5 7.4 %all-to-all-start.2 = ((f32[32,1,3072]{2,1,0:T(1,128)}), f32[32,1,3072]{2,1,0:T(1,128)S(1)}, u32[]{:S(2)}, u32[]{:S(2)}) async-start(f32[32,1,3072]{2,1,0:T(1,128)} %reshape.162), calls=%async_computation.2 | async-start | bytes 786432 | tf_op jit(solution)/shard_map/all_to_all | solution.py:164
  45.1 10.2 %all-to-all-done.2 = f32[32,1,3072]{2,1,0:T(1,128)S(1)} async-done(((f32[32,1,3072]{2,1,0:T(1,128)}), f32[32,1,3072]{2,1,0:T(1,128)S(1)}, u32[]{:S(2)}, u32[]{:S(2)}) %all-to-all-start.2) | async-done | bytes 393248 | tf_op jit(solution)/shard_map/all_to_all | solution.py:164
  55.2 13.0 %all-to-all-start = ((f32[16,1,4096]{2,1,0:T(1,128)}), f32[16,1,4096]{2,1,0:T(1,128)S(1)}, u32[]{:S(2)}, u32[]{:S(2)}) async-start(f32[16,1,4096]{2,1,0:T(1,128)} %reshape.160), calls=%async_computation | async-start | bytes 524288 | tf_op jit(solution)/shard_map/all_to_all | solution.py:120
  68.8 1.5 reduce.3
  72.2 4.4 %while.36 = (s32[]{:T(128)}, f32[2,32,1024]{2,1,0:T(8,128)S(1)}, f32[6,256,2,32]{1,0,3,2:T(8,128)S(1)}, s32[6,256]{1,0:T(8,128)S(1)}, s32[]{:T(128)}, /*index=5*/s32[]{:T(128)}) while((s32[]{:T(128)}, f32[2,32,1024]{2,1,0:T(8,128)S(1)}, f32[6,256,2,32]{1,0,3,2:T(8,128)S(1)}, s32[6,256]{1,0:T(8,128)S(1)}, s32[]{:T(128)}, ...), condition=%wide.region_2.3_spmd.clone, body=%wide.region_1.2_spmd.clone.sunk | while | flops 201719808 | bytes 724055 | solution.py:88
  76.6 6.3 %all-to-all-done = f32[16,1,4096]{2,1,0:T(1,128)S(1)} async-done(((f32[16,1,4096]{2,1,0:T(1,128)}), f32[16,1,4096]{2,1,0:T(1,128)S(1)}, u32[]{:S(2)}, u32[]{:S(2)}) %all-to-all-start) | async-done | bytes 262176 | tf_op jit(solution)/shard_map/all_to_all | solution.py:120
  82.8 9.8 %all-to-all-start.5 = ((f32[16,1,4096]{2,1,0:T(1,128)}), f32[16,1,4096]{2,1,0:T(1,128)}, u32[]{:S(2)}, u32[]{:S(2)}) async-start(f32[16,1,4096]{2,1,0:T(1,128)} %reshape.166), calls=%async_computation.5 | async-start | bytes 524288 | tf_op jit(solution)/shard_map/all_to_all | solution.py:195
  92.7 1.2 reduce.2
  93.9 2.8 %reshape.161 = f32[1024,2,2,16]{3,2,1,0:T(2,128)S(1)} reshape(f32[16,4096]{1,0:T(8,128)S(1)} %reduce.2) | data formatting | bytes 524288
  96.7 2.4 %copy.48 = f32[2,16,2,16,64]{4,3,2,1,0:T(8,128)} copy(f32[2,16,2,16,64]{3,2,0,4,1:T(2,128)S(1)} %bitcast.114) | data formatting | bytes 524288 | tf_op jit(solution)/shard_map/all_to_all | solution.py:120
  99.2 1.2 reshape.143
  100.4 20.1 %while.37 = (s32[]{:T(128)}, f32[2,32,1024]{2,1,0:T(8,128)S(1)}, s32[16,64]{1,0:T(8,128)S(1)}, f32[16,32,32]{2,1,0:T(8,128)}, f32[2,32,1024]{2,1,0:T(8,128)S(1)}, /*index=5*/s32[]{:T(128)}, s32[]{:T(128)}) while((s32[]{:T(128)}, f32[2,32,1024]{2,1,0:T(8,128)S(1)}, s32[16,64]{1,0:T(8,128)S(1)}, f32[16,32,32]{2,1,0:T(8,128)}, ...), condition=%wide.region_4.5_spmd.clone, body=%wide.region_3.4_spmd.clone.sunk | while | flops 25363460 | bytes 811611 | solution.py:181
  100.5 1.1 fusion.58
  101.8 1.1 fusion.58
  103.0 1.1 fusion.58
  104.3 1.1 fusion.58
  105.5 1.1 fusion.58
  106.8 1.1 fusion.58
  108.0 1.1 fusion.58
  109.3 1.1 fusion.58
  110.5 1.1 fusion.58
  111.8 1.1 fusion.58
  113.1 1.1 fusion.58
  114.3 1.1 fusion.58
  115.6 1.1 fusion.58
  116.8 1.1 fusion.58
  118.1 1.1 fusion.58
  119.3 1.1 fusion.58
  120.5 5.4 %while.35 = (s32[]{:T(128)}, f32[6,256,2]{1,0,2:T(8,128)S(1)}, f32[6,256,2,32]{1,0,3,2:T(8,128)S(1)}, s32[6,256]{1,0:T(8,128)S(1)}, f32[2,32,1024]{2,1,0:T(8,128)S(1)}, /*index=5*/s32[]{:T(128)}, s32[]{:T(128)}) while((s32[]{:T(128)}, f32[6,256,2]{1,0,2:T(8,128)S(1)}, f32[6,256,2,32]{1,0,3,2:T(8,128)S(1)}, s32[6,256]{1,0:T(8,128)S(1)}, ...), condition=%wide.region_7.8_spmd, body=%wide.region_5.7_spmd.sunk | while | flops 201620992 | bytes 472153 | solution.py:104
  126.7 4.2 %all-to-all-start.6 = ((f32[32,48,2]{1,2,0:T(2,128)}), f32[32,48,2]{1,2,0:T(2,128)S(1)}, u32[]{:S(2)}, u32[]{:S(2)}) async-start(f32[32,48,2]{1,2,0:T(2,128)} %copy.61), calls=%async_computation.6 | async-start | bytes 65536 | tf_op jit(solution)/shard_map/all_to_all | solution.py:186
  132.5 5.8 %all-to-all-done.6 = f32[32,48,2]{1,2,0:T(2,128)S(1)} async-done(((f32[32,48,2]{1,2,0:T(2,128)}), f32[32,48,2]{1,2,0:T(2,128)S(1)}, u32[]{:S(2)}, u32[]{:S(2)}) %all-to-all-start.6) | async-done | bytes 12320 | tf_op jit(solution)/shard_map/all_to_all | solution.py:186
  138.3 11.7 %all-to-all-start.4 = ((f32[16,1,4096]{2,1,0:T(1,128)}), f32[16,1,4096]{2,1,0:T(1,128)S(1)}, u32[]{:S(2)}, u32[]{:S(2)}) async-start(f32[16,1,4096]{2,1,0:T(1,128)} %reshape.164), calls=%async_computation.4 | async-start | bytes 524288 | tf_op jit(solution)/shard_map/all_to_all | solution.py:194
  150.2 2.2 %reduce.5 = f32[16,4096]{1,0:T(8,128)S(1)} reduce(f32[16,1,4096]{2,1,0:T(1,128)} %all-to-all-done.5, f32[]{:T(128)} %broadcast.190), dimensions={1}, to_apply=%all_to_all.68.reduce_sub_computation | reduce | bytes 524292 | tf_op jit(solution)/shard_map/all_to_all | solution.py:195
  153.2 10.8 %all-to-all-done.4 = f32[16,1,4096]{2,1,0:T(1,128)S(1)} async-done(((f32[16,1,4096]{2,1,0:T(1,128)}), f32[16,1,4096]{2,1,0:T(1,128)S(1)}, u32[]{:S(2)}, u32[]{:S(2)}) %all-to-all-start.4) | async-done | bytes 262176 | tf_op jit(solution)/shard_map/all_to_all | solution.py:194
  164.0 1.2 reduce.4
  166.0 7.3 %collective-permute-start = (f32[4,2,3,1024]{3,2,1,0:T(4,128)S(1)}, f32[4,2,3,1024]{3,2,1,0:T(4,128)S(1)}, u32[]{:S(2)}, u32[]{:S(2)}) collective-permute-start(f32[4,2,3,1024]{3,2,1,0:T(4,128)S(1)} %get-tuple-element.295), channel_id=1, source_target_pairs={{0,1},{1,2},{2,3},{3,4},{4,5},{5,6},{6,7},{7,8},{8,9},{9,10},{10,1... | collective-permute-start | bytes 294920 | tf_op jit(solution)/shard_map/ppermute | solution.py:14
  173.3 2.1 %collective-permute-start.1 = (f32[4,2,3,1024]{3,2,1,0:T(4,128)S(1)}, f32[4,2,3,1024]{3,2,1,0:T(4,128)S(1)}, u32[]{:S(2)}, u32[]{:S(2)}) collective-permute-start(f32[4,2,3,1024]{3,2,1,0:T(4,128)S(1)} %get-tuple-element.296), channel_id=1, source_target_pairs={{1,0},{2,1},{3,2},{4,3},{5,4},{6,5},{7,6},{8,7},{9,8},{10,9},{11,1... | collective-permute-start | bytes 294920 | tf_op jit(solution)/shard_map/ppermute | solution.py:17
  175.5 1.6 fusion.27
  177.1 2.5 %collective-permute-done.1 = f32[4,2,3,1024]{3,2,1,0:T(4,128)S(1)} collective-permute-done((f32[4,2,3,1024]{3,2,1,0:T(4,128)S(1)}, f32[4,2,3,1024]{3,2,1,0:T(4,128)S(1)}, u32[]{:S(2)}, u32[]{:S(2)}) %collective-permute-start.1) | collective-permute-done | bytes 98336 | tf_op jit(solution)/shard_map/ppermute | solution.py:17
  (158 shorter events, 25.5 us)
Async XLA Ops:
  0.6 27.0 %copy-start = (f32[1,1,512,64]{2,3,1,0:T(8,128)S(1)}, f32[1,1,512,64]{2,3,1,0:T(8,128)}, u32[]{:S(2)}) copy-start(f32[1,1,512,64]{2,3,1,0:T(8,128)} %param.19) | copy-start | bytes 393220
  1.3 1.0 copy-start.4
  3.1 27.3 %copy-start.1 = (f32[2,2,16,1024]{3,2,1,0:T(8,128)S(1)}, f32[2,2,16,1024]{3,2,1,0:T(8,128)}, u32[]{:S(2)}) copy-start(f32[2,2,16,1024]{3,2,1,0:T(8,128)} %param.15) | copy-start | bytes 786436
  6.0 17.3 %all-to-all-start.3 = ((f32[32,48,1]{1,2,0:T(1,128)}), f32[32,48,1]{1,2,0:T(1,128)S(1)}, u32[]{:S(2)}, u32[]{:S(2)}) async-start(f32[32,48,1]{1,2,0:T(1,128)} %all_to_all.62), calls=%async_computation.3 | async-start | bytes 32768 | tf_op jit(solution)/shard_map/all_to_all | solution.py:166
  23.4 14.1 %all-to-all-start.1 = ((f32[32,48,2]{1,2,0:T(2,128)}), f32[32,48,2]{1,2,0:T(2,128)S(1)}, u32[]{:S(2)}, u32[]{:S(2)}) async-start(f32[32,48,2]{1,2,0:T(2,128)} %fusion.14), calls=%async_computation.1 | async-start | bytes 65536 | tf_op jit(solution)/shard_map/all_to_all | solution.py:165
  37.5 17.7 %all-to-all-start.2 = ((f32[32,1,3072]{2,1,0:T(1,128)}), f32[32,1,3072]{2,1,0:T(1,128)S(1)}, u32[]{:S(2)}, u32[]{:S(2)}) async-start(f32[32,1,3072]{2,1,0:T(1,128)} %reshape.162), calls=%async_computation.2 | async-start | bytes 786432 | tf_op jit(solution)/shard_map/all_to_all | solution.py:164
  55.2 27.6 %all-to-all-start = ((f32[16,1,4096]{2,1,0:T(1,128)}), f32[16,1,4096]{2,1,0:T(1,128)S(1)}, u32[]{:S(2)}, u32[]{:S(2)}) async-start(f32[16,1,4096]{2,1,0:T(1,128)} %reshape.160), calls=%async_computation | async-start | bytes 524288 | tf_op jit(solution)/shard_map/all_to_all | solution.py:120
  82.8 43.9 %all-to-all-start.5 = ((f32[16,1,4096]{2,1,0:T(1,128)}), f32[16,1,4096]{2,1,0:T(1,128)}, u32[]{:S(2)}, u32[]{:S(2)}) async-start(f32[16,1,4096]{2,1,0:T(1,128)} %reshape.166), calls=%async_computation.5 | async-start | bytes 524288 | tf_op jit(solution)/shard_map/all_to_all | solution.py:195
  96.7 3.7 %copy-start.2 = (s32[16,64]{1,0:T(8,128)S(1)}, s32[16,64]{1,0:T(8,128)}, u32[]{:S(2)}) copy-start(s32[16,64]{1,0:T(8,128)} %param.17) | copy-start | bytes 12292
  100.4 20.1 %copy-start.3 = (f32[6,256,2]{1,0,2:T(8,128)S(1)}, f32[6,256,2]{1,0,2:T(8,128)}, u32[]{:S(2)}) copy-start(f32[6,256,2]{1,0,2:T(8,128)} %custom-call.3) | copy-start | bytes 36868
  126.7 11.6 %all-to-all-start.6 = ((f32[32,48,2]{1,2,0:T(2,128)}), f32[32,48,2]{1,2,0:T(2,128)S(1)}, u32[]{:S(2)}, u32[]{:S(2)}) async-start(f32[32,48,2]{1,2,0:T(2,128)} %copy.61), calls=%async_computation.6 | async-start | bytes 65536 | tf_op jit(solution)/shard_map/all_to_all | solution.py:186
  138.3 25.7 %all-to-all-start.4 = ((f32[16,1,4096]{2,1,0:T(1,128)}), f32[16,1,4096]{2,1,0:T(1,128)S(1)}, u32[]{:S(2)}, u32[]{:S(2)}) async-start(f32[16,1,4096]{2,1,0:T(1,128)} %reshape.164), calls=%async_computation.4 | async-start | bytes 524288 | tf_op jit(solution)/shard_map/all_to_all | solution.py:194
  165.2 10.3 %copy-start.5 = (pred[512]{0:T(512)(128)(4,1)S(1)}, pred[512]{0:T(512)(128)(4,1)}, u32[]{:S(2)}) copy-start(pred[512]{0:T(512)(128)(4,1)} %copy-done.4) | copy-start | bytes 1540
  166.0 11.1 %collective-permute-start = (f32[4,2,3,1024]{3,2,1,0:T(4,128)S(1)}, f32[4,2,3,1024]{3,2,1,0:T(4,128)S(1)}, u32[]{:S(2)}, u32[]{:S(2)}) collective-permute-start(f32[4,2,3,1024]{3,2,1,0:T(4,128)S(1)} %get-tuple-element.295), channel_id=1, source_target_pairs={{0,1},{1,2},{2,3},{3,4},{4,5},{5,6},{6,7},{7,8},{8,9},{9,10},{10,1... | collective-permute-start | bytes 294920 | tf_op jit(solution)/shard_map/ppermute | solution.py:14
  173.3 6.3 %collective-permute-start.1 = (f32[4,2,3,1024]{3,2,1,0:T(4,128)S(1)}, f32[4,2,3,1024]{3,2,1,0:T(4,128)S(1)}, u32[]{:S(2)}, u32[]{:S(2)}) collective-permute-start(f32[4,2,3,1024]{3,2,1,0:T(4,128)S(1)} %get-tuple-element.296), channel_id=1, source_target_pairs={{1,0},{2,1},{3,2},{4,3},{5,4},{6,5},{7,6},{8,7},{9,8},{10,9},{11,1... | collective-permute-start | bytes 294920 | tf_op jit(solution)/shard_map/ppermute | solution.py:17
where the time goes:
time: 187 us; the launch traced here: 183 us
  starting transfers between devices  70.2 us (38%)
  waiting for transfers between devices  38.8 us (21%)
  matrix products  36.2 us (19%)
  local copies, waits for them, and re-layouts  25.1 us (13%)
  other arithmetic  10.1 us (5%)
  between operations  1.87 us (1%)
    dot_general x16, matrix products, mix_class(): jnp.einsum('kj,tkn->tjn', matrix, adj_mixed, precision=lax.Precision.HIGH...  18.2 us
    all_to_all x1, starting transfers between devices, per_device(): lax.all_to_all(adjoint_in, 'lev', split_axis=3, concat_axis=1, tiled=True)  13 us
    unnamed x23, local copies, waits for them, and re-layouts  12.8 us
    all_to_all x1, starting transfers between devices, per_device(): lax.all_to_all(adj_grid, 'lev', split_axis=1, concat_axis=3, tiled=True)  11.7 us
    all_to_all x1, waiting for transfers between devices, per_device(): lax.all_to_all(adj_grid, 'lev', split_axis=1, concat_axis=3, tiled=True)  10.8 us
    all_to_all x1, starting transfers between devices, per_device(): lax.all_to_all(buf_place, 'lat', split_axis=0, concat_axis=0, tiled=True)  10.4 us
    all_to_all x1, waiting for transfers between devices, per_device(): lax.all_to_all(buf_kernels, 'lat', split_axis=0, concat_axis=0, tiled=True)  10.2 us
    all_to_all x1, starting transfers between devices, per_device(): lax.all_to_all(courant, 'lev', split_axis=1, concat_axis=3, tiled=True)  9.85 us
  transfers between devices with their start and end apart: 9, of which 6 were waited for; matrix products, arithmetic and copies ran while one was open for 33% of the time, Pallas kernels for 0%

commit v1 on v0

v1 whole, which is shorter than its diff:
```python
import functools

import jax
import jax.numpy as jnp
from jax import lax
from jax.experimental import pallas as pl
from jax.experimental.pallas import tpu as pltpu
from jax.sharding import PartitionSpec as P

MESH = pl.DeviceIdType.MESH
F32, BF16, I32 = jnp.float32, jnp.bfloat16, jnp.int32
ROWS = 16
TILES = 8
HALF = 64
MSG = 8


def lanes(shape):
    return lax.broadcasted_iota(I32, shape, len(shape) - 1)


def turn(x, shift):
    shift = shift % 128
    return x if shift == 0 else pltpu.roll(x, shift, x.ndim - 1)


def low_half(shape):
    return lanes(shape) < HALF


def pair(a, b):
    low = low_half(a.shape)
    return jnp.where(low, a, turn(b, HALF)), jnp.where(low, turn(a, HALF), b)


def split(x):
    high = x.astype(BF16)
    return high, (x - high.astype(F32)).astype(BF16)


def dot(a, b, contract=(1, 0)):
    return lax.dot_general(
        a, b, (((contract[0],), (contract[1],)), ((), ())), preferred_element_type=F32
    )


def one_hot(mask):
    return jnp.where(mask, 1.0, 0.0).astype(BF16)


def pack_lon(tiles):
    x = lanes(tiles[0].shape) % HALF
    to_west, to_east = tiles[0], turn(tiles[0], 66)
    for p in range(1, TILES):
        here = x // 2 == p
        to_west = jnp.where(here, turn(tiles[p], 2 * p), to_west)
        to_east = jnp.where(here, turn(tiles[p], 2 * p + 66), to_east)
    return to_west, to_east


def shift_lon(tile, p, from_west, from_east, steps):
    x = lanes(tile.shape) % HALF
    east = turn(from_east, HALF - 2 * p)
    west = turn(from_west, 126 - 2 * p)
    out = []
    for d in steps:
        if d > 0:
            out.append(turn(jnp.where(x < d, east, tile), -d))
        else:
            out.append(turn(jnp.where(x >= HALF + d, west, tile), -d))
    return out


def pack_lat(tiles):
    low = low_half(tiles[0].shape)
    to_south = jnp.where(low, tiles[0], turn(tiles[1], HALF))
    to_north = jnp.where(low, turn(tiles[6], HALF), tiles[7])
    return to_south, to_north


def extend_lat(tiles, from_south, from_north):
    low = low_half(tiles[0].shape)
    return (
        [
            jnp.where(low, from_south, turn(tiles[6], HALF)),
            turn(jnp.where(low, tiles[7], from_south), HALF),
        ]
        + list(tiles)
        + [
            turn(jnp.where(low, from_north, tiles[0]), HALF),
            jnp.where(low, turn(tiles[1], HALF), from_north),
        ]
    )


def face_weights(before, here, after, after2):
    def parts(c):
        pos, neg = jnp.maximum(c, 0.0), jnp.minimum(c, 0.0)
        return pos, neg, 0.25 * pos * (1.0 - pos), 0.25 * neg * (1.0 + neg)

    _, _, _, sn_before = parts(before)
    _, neg_here, sp_here, _ = parts(here)
    pos_after, _, _, sn_after = parts(after)
    _, _, sp_after2, _ = parts(after2)
    own = neg_here + sp_here
    nxt = pos_after + sn_after
    return sn_before, -own - sn_before, own - nxt, nxt + sp_after2, -sp_after2


def kernel(
    n_lev,
    n_lat,
    adj_hbm,
    cour_hbm,
    top_hbm,
    mat_hbm,
    kern_hbm,
    wt_hbm,
    owner_hbm,
    cell_hbm,
    count_hbm,
    out_hbm,
    sens_hbm,
    adj_in,
    cour_in,
    top_in,
    mat_in,
    kern_in,
    wt_in,
    owner_in,
    cell_in,
    count_in,
    out_vm,
    sens_vm,
    fwd_out,
    fwd_in,
    back_out,
    back_in,
    msg_out,
    msg_in,
    ret_out,
    ret_in,
    c_lon_out,
    c_lon_in,
    c_lat_out,
    c_lat_in,
    a_lon_out,
    a_lon_in,
    a_lat_out,
    a_lat_in,
    place,
    payload,
    kern_rows,
    weighted,
    hot,
    deposit,
    cour_t,
    weights,
    mix,
    conv,
    conv_split,
    ret_split,
    in_sem,
    out_sem,
    fwd_send,
    fwd_recv,
    back_send,
    back_recv,
    msg_send,
    msg_recv,
    ret_send,
    ret_recv,
    c_send,
    c_recv,
    a_send,
    a_recv,
):
    lev, lat = lax.axis_index("lev"), lax.axis_index("lat")
    levels = 2 * n_lev
    slots = owner_in.shape[1]

    def lev_at(d):
        return lax.rem(lev + d + n_lev, n_lev)

    def lat_at(d):
        return lax.rem(lat + d + n_lat, n_lat)

    loads = [
        pltpu.make_async_copy(source, target, in_sem.at[i])
        for i, (source, target) in enumerate(
            [
                (adj_hbm, adj_in),
                (owner_hbm, owner_in),
                (cell_hbm, cell_in),
                (count_hbm, count_in),
                (kern_hbm, kern_in),
                (wt_hbm, wt_in),
                (cour_hbm, cour_in),
                (top_hbm, top_in),
                (mat_hbm, mat_in),
            ]
        )
    ]
    for load in loads:
        load.start()

    barrier = pltpu.get_barrier_semaphore()

    def greet_lev(d, _):
        pl.semaphore_signal(barrier, inc=1, device_id={"lev": lev_at(d)}, device_id_type=MESH)
        return _

    def greet_lat(d, _):
        pl.semaphore_signal(barrier, inc=1, device_id={"lat": lat_at(d)}, device_id_type=MESH)
        return _

    lax.fori_loop(1, n_lev, greet_lev, 0)
    lax.fori_loop(1, n_lat, greet_lat, 0)

    loads[0].wait()
    for t in range(2):
        for m in range(n_lev // 2):
            for kk in range(2):
                cols = pl.ds(m * 128, 128)
                a, b = pair(adj_in[t, kk, 0:8, cols], adj_in[t, kk, 8:16, cols])
                fwd_out[t, pl.ds(m * 32 + kk * 8, 8), :] = a
                fwd_out[t, pl.ds(m * 32 + 16 + kk * 8, 8), :] = b
    pl.semaphore_wait(barrier, n_lev + n_lat - 2)

    def block(i):
        return pl.ds(pl.multiple_of(i * 16, 16), 16)

    def fwd_copy(t, d):
        return pltpu.make_async_remote_copy(
            src_ref=fwd_out.at[t, block(lev_at(d)), :],
            dst_ref=fwd_in.at[t, block(lev), :],
            send_sem=fwd_send.at[t, d],
            recv_sem=fwd_recv.at[t, d],
            device_id={"lev": lev_at(d)},
            device_id_type=MESH,
        )

    def start_fwd(t):
        def step(d, _):
            fwd_copy(t, d).start()
            return _

        lax.fori_loop(1, n_lev, step, 0)

    start_fwd(0)
    start_fwd(1)
    for t in range(2):
        fwd_in[t, block(lev), :] = fwd_out[t, block(lev), :]

    for i in range(1, 6):
        loads[i].wait()
    owner, cell = owner_in[...], cell_in[...]
    valid = lanes((1, slots)) < count_in[...]
    owned = (lax.broadcasted_iota(I32, (n_lat, slots), 0) == owner) & valid
    upper = one_hot(lax.broadcasted_iota(I32, (slots, slots), 0) < lanes((slots, slots)))
    before = dot(one_hot(owned), upper)
    rank = jnp.sum(jnp.where(owned, before, 0.0), axis=0, keepdims=True).astype(I32)
    slot = jnp.where(valid, owner * HALF + rank, -1)
    row = cell // HALF
    packed = (row % TILES) * 128 + (row // TILES) * HALF + cell % HALF
    payload[...] = jnp.zeros((slots, 128), F32)
    payload[:, 0 : 2 * levels] = kern_in[...]
    payload[:, HALF : HALF + 2] = wt_in[...]
    turned = jnp.transpose(payload[...])
    small = turned[HALF : HALF + MSG, :]
    small = jnp.where(
        lax.broadcasted_iota(I32, (MSG, slots), 0) == 2, (packed + 1).astype(F32), small
    )
    table = jnp.concatenate([turned[0 : 2 * levels, :], small], axis=0)
    tall = 2 * levels + MSG
    table = jnp.concatenate(split(table), axis=0)

    def route(q, _):
        base = pl.multiple_of(q * 256, 256)
        spot = lax.broadcasted_iota(I32, (256, slots), 0) + base
        hits = one_hot(spot == slot)
        place[pl.ds(base, 256), :] = hits
        sent = dot(table, hits, (1, 1))
        sent = sent[:tall] + sent[tall:]
        for m in range(2):
            part = sent[:, m * 128 : (m + 1) * 128]
            a, b = pair(part[:levels], part[levels : 2 * levels])
            rest = part[2 * levels :]
            msg_out[q * 4 + m * 2, 0:levels, :] = a
            msg_out[q * 4 + m * 2 + 1, 0:levels, :] = b
            msg_out[q * 4 + m * 2, levels : levels + MSG, :] = rest
            msg_out[q * 4 + m * 2 + 1, levels : levels + MSG, :] = turn(rest, HALF)
        return _

    lax.fori_loop(0, n_lat // 4, route, 0)

    def msg_copy(d):
        return pltpu.make_async_remote_copy(
            src_ref=msg_out.at[lat_at(d)],
            dst_ref=msg_in.at[lat],
            send_sem=msg_send.at[d],
            recv_sem=msg_recv.at[d],
            device_id={"lat": lat_at(d)},
            device_id_type=MESH,
        )

    def start_msg(d, _):
        msg_copy(d).start()
        return _

    lax.fori_loop(1, n_lat, start_msg, 0)
    msg_in[lat] = msg_out[lat]

    loads[6].wait()
    for c in range(2):
        for p in range(TILES):
            a = cour_in[c, pl.ds(p, levels, stride=ROWS), :]
            b = cour_in[c, pl.ds(p + TILES, levels, stride=ROWS), :]
            cour_t[c, p] = jnp.concatenate([a, b], axis=1)
    c_lon_out[0], c_lon_out[1] = pack_lon([cour_t[0, p] for p in range(TILES)])
    c_lat_out[0], c_lat_out[1] = pack_lat([cour_t[1, p] for p in range(TILES)])

    def edge_copies(lon_out, lon_in, lat_out, lat_in, send, recv):
        copies = []
        for i, step in enumerate((-1, 1)):
            copies.append(
                pltpu.make_async_remote_copy(
                    src_ref=lon_out.at[i],
                    dst_ref=lon_in.at[i],
                    send_sem=send.at[i],
                    recv_sem=recv.at[i],
                    device_id={"lev": lev_at(step)},
                    device_id_type=MESH,
                )
            )
        for i, step in enumerate((-1, 1)):
            copies.append(
                pltpu.make_async_remote_copy(
                    src_ref=lat_out.at[i],
                    dst_ref=lat_in.at[i],
                    send_sem=send.at[2 + i],
                    recv_sem=recv.at[2 + i],
                    device_id={"lat": lat_at(step)},
                    device_id_type=MESH,
                )
            )
        return copies

    c_copies = edge_copies(c_lon_out, c_lon_in, c_lat_out, c_lat_in, c_send, c_recv)
    for copy in c_copies:
        copy.start()

    loads[7].wait()
    loads[8].wait()
    for g in range(mat_in.shape[0] // 2):
        wide = []
        for odd in range(2):
            high, low = split(jnp.transpose(mat_in[2 * g + odd]))
            wide += [high, high, low]
        mix[pl.ds(g * levels, levels), :] = jnp.concatenate(wide, axis=1)
    tops = jnp.concatenate([top_in[0:8, :], top_in[8:16, :]], axis=1)

    first, last = lat == 0, lat == n_lat - 1
    for copy in c_copies:
        copy.wait()
    from_east, from_west = c_lon_in[0], c_lon_in[1]
    from_north, from_south = c_lat_in[0], c_lat_in[1]
    from_north = jnp.where(last, 0.0, from_north)
    from_south = jnp.where(first, 0.0, from_south)
    rows_c = [cour_t[1, p] for p in range(TILES)]
    rows_c[0] = jnp.where(low_half(rows_c[0].shape) & first, 0.0, rows_c[0])
    rows_c = extend_lat(rows_c, from_south, from_north)
    for p in range(TILES):
        here = cour_t[0, p]
        before_x, after_x, after2_x = shift_lon(here, p, from_west, from_east, (-1, 1, 2))
        lon_w = face_weights(before_x, here, after_x, after2_x)
        lat_w = face_weights(rows_c[p + 1], rows_c[p + 2], rows_c[p + 3], rows_c[p + 4])
        weights[p, 0] = 1.0 + lon_w[2] + lat_w[2]
        for i, j in enumerate((0, 1, 3, 4)):
            weights[p, 1 + i] = lon_w[j]
            weights[p, 5 + i] = lat_w[j]

    def wait_msg(d, _):
        msg_copy(d).wait()
        return _

    lax.fori_loop(1, n_lat, wait_msg, 0)
    columns = TILES * 128

    def arrive(m, _):
        a, b = msg_in[2 * m], msg_in[2 * m + 1]
        one, two = pair(a[:levels], b[:levels])
        rest, _unused = pair(a[levels:], b[levels:])
        kern_rows[m, 0:levels, :] = one
        kern_rows[m, levels : 2 * levels, :] = two
        wk = jnp.concatenate([one * rest[0:1], two * rest[1:2]], axis=0)
        at = pl.ds(pl.multiple_of(m * 128, 128), 128)
        high, low = split(wk)
        weighted[0 : 2 * levels, at] = high
        weighted[2 * levels :, at] = low
        target = rest[2:3].astype(I32) - 1
        hot[:, at] = one_hot(lax.broadcasted_iota(I32, (columns, 128), 0) == target)
        return _

    lax.fori_loop(0, n_lat // 2, arrive, 0)
    for q in range(TILES // 2):
        got = dot(weighted[...], hot[pl.ds(q * 256, 256), :], (1, 1))
        got = got[: 2 * levels] + got[2 * levels :]
        for t in range(2):
            for i in range(2):
                deposit[t, 2 * q + i] = got[
                    t * levels : (t + 1) * levels, i * 128 : (i + 1) * 128
                ]

    def wait_fwd(t):
        def step(d, _):
            fwd_copy(t, d).wait()
            return _

        lax.fori_loop(1, n_lev, step, 0)

    for t in range(2):
        wait_fwd(t)
        for q in range(TILES // 2):
            x = jnp.concatenate(
                [
                    fwd_in[t, pl.ds(p, levels, stride=TILES), :] + deposit[t, p]
                    for p in (2 * q, 2 * q + 1)
                ],
                axis=1,
            )
            top = jnp.concatenate([tops[2 * q : 2 * q + 1], tops[2 * q + 1 : 2 * q + 2]], axis=1)
            stack = []
            for odd in range(2):
                high, low = split(jnp.where(top % 2 == odd, x, 0.0))
                stack += [high, low, high]
            mixed = dot(mix[...], jnp.concatenate(stack, axis=0))
            result = mixed[0:levels]
            for g in range(1, mat_in.shape[0] // 2):
                result = jnp.where(top // 2 == g, mixed[g * levels : (g + 1) * levels], result)
            high, low = split(result)
            conv_split[pl.ds(t * levels, levels), pl.ds(q * 256, 256)] = high
            conv_split[pl.ds((2 + t) * levels, levels), pl.ds(q * 256, 256)] = low
            conv[t, 2 * q] = result[:, :128]
            conv[t, 2 * q + 1] = result[:, 128:]
        tiles = [conv[t, p] for p in range(TILES)]
        rows_t = pl.ds(t * levels, levels)
        a_lon_out[0, rows_t, :], a_lon_out[1, rows_t, :] = pack_lon(tiles)
        a_lat_out[0, rows_t, :], a_lat_out[1, rows_t, :] = pack_lat(tiles)
    a_copies = edge_copies(a_lon_out, a_lon_in, a_lat_out, a_lat_in, a_send, a_recv)
    for copy in a_copies:
        copy.start()
    for copy in a_copies:
        copy.wait()

    def back_copy(t, d):
        return pltpu.make_async_remote_copy(
            src_ref=back_out.at[t, block(lev_at(d)), :],
            dst_ref=back_in.at[t, block(lev), :],
            send_sem=back_send.at[t, d],
            recv_sem=back_recv.at[t, d],
            device_id={"lev": lev_at(d)},
            device_id_type=MESH,
        )

    for t in range(2):
        rows_t = pl.ds(t * levels, levels)
        from_east, from_west = a_lon_in[0, rows_t, :], a_lon_in[1, rows_t, :]
        from_north, from_south = a_lat_in[0, rows_t, :], a_lat_in[1, rows_t, :]
        from_north = jnp.where(last, 0.0, from_north)
        from_south = jnp.where(first, 0.0, from_south)
        tiles = extend_lat([conv[t, p] for p in range(TILES)], from_south, from_north)
        for p in range(TILES):
            here = tiles[p + 2]
            around = shift_lon(here, p, from_west, from_east, (-2, -1, 1, 2))
            around += [tiles[p], tiles[p + 1], tiles[p + 3], tiles[p + 4]]
            total = weights[p, 0] * here
            for i in range(8):
                total = total + weights[p, 1 + i] * around[i]
            back_out[t, pl.ds(p, levels, stride=TILES), :] = total

        def start_back(d, _, t=t):
            back_copy(t, d).start()
            return _

        lax.fori_loop(1, n_lev, start_back, 0)
        back_in[t, block(lev), :] = back_out[t, block(lev), :]

    for m in range(n_lat // 4):
        picked = dot(conv_split[...], hot[:, pl.ds(m * 256, 256)])
        picked = picked[: 2 * levels] + picked[2 * levels :]
        for i in range(2):
            product = picked[:, i * 128 : (i + 1) * 128] * kern_rows[2 * m + i]
            sums = [
                jnp.sum(product[t * levels : (t + 1) * levels], axis=0, keepdims=True)
                for t in range(2)
            ]
            which = lax.broadcasted_iota(I32, (MSG, 128), 0)
            both = jnp.where(which == 0, sums[0], jnp.where(which == 1, sums[1], 0.0))
            ret_out[4 * m + 2 * i] = both
            ret_out[4 * m + 2 * i + 1] = turn(both, HALF)

    def ret_copy(d):
        return pltpu.make_async_remote_copy(
            src_ref=ret_out.at[lat_at(d)],
            dst_ref=ret_in.at[lat],
            send_sem=ret_send.at[d],
            recv_sem=ret_recv.at[d],
            device_id={"lat": lat_at(d)},
            device_id_type=MESH,
        )

    def start_ret(d, _):
        ret_copy(d).start()
        return _

    def wait_ret(d, _):
        ret_copy(d).wait()
        return _

    lax.fori_loop(1, n_lat, start_ret, 0)
    ret_in[lat] = ret_out[lat]
    lax.fori_loop(1, n_lat, wait_ret, 0)
    for m in range(n_lat // 2):
        both, _unused = pair(ret_in[2 * m], ret_in[2 * m + 1])
        ret_split[:, pl.ds(m * 128, 128)] = jnp.concatenate(split(both), axis=0)
    own = dot(ret_split[...], place[...])
    own = own[:MSG] + own[MSG:]
    sens_vm[...] = jnp.transpose(own)[:, 0:2]
    sens_store = pltpu.make_async_copy(sens_vm, sens_hbm, out_sem.at[0])
    sens_store.start()

    for t in range(2):

        def wait_back(d, _, t=t):
            back_copy(t, d).wait()
            return _

        lax.fori_loop(1, n_lev, wait_back, 0)
        for m in range(n_lev // 2):
            for kk in range(2):
                a, b = pair(
                    back_in[t, pl.ds(m * 32 + kk * 8, 8), :],
                    back_in[t, pl.ds(m * 32 + 16 + kk * 8, 8), :],
                )
                out_vm[t, kk, 0:8, pl.ds(m * 128, 128)] = a
                out_vm[t, kk, 8:16, pl.ds(m * 128, 128)] = b
    out_store = pltpu.make_async_copy(out_vm, out_hbm, out_sem.at[1])
    out_store.start()
    out_store.wait()
    sens_store.wait()


def per_device(
    n_lev,
    n_lat,
    adjoint_in,
    courant,
    cloud_top,
    conv_inverse,
    sounding_kernel,
    sounding_weight,
    sounding_owner,
    sounding_cell,
    sounding_count,
):
    levels = 2 * n_lev
    slots = sounding_kernel.shape[2]
    classes = conv_inverse.shape[0]
    columns = TILES * 128
    spots = n_lat * HALF
    operands = (
        adjoint_in,
        courant.reshape(2, levels * ROWS, HALF),
        cloud_top,
        conv_inverse,
        sounding_kernel.reshape(slots, 2 * levels),
        sounding_weight.reshape(slots, 2),
        sounding_owner.reshape(1, slots),
        sounding_cell.reshape(1, slots),
        sounding_count,
    )
    vm, dma = pltpu.VMEM, pltpu.SemaphoreType.DMA
    scratch = [vm(x.shape, x.dtype) for x in operands]
    scratch += [
        vm(adjoint_in.shape, F32),
        vm((slots, 2), F32),
    ]
    scratch += [vm((2, n_lev * 16, 128), F32) for _ in range(4)]
    scratch += [vm((n_lat, levels + MSG, 128), F32) for _ in range(2)]
    scratch += [vm((n_lat, MSG, 128), F32) for _ in range(2)]
    scratch += [vm((2, levels, 128), F32) for _ in range(4)]
    scratch += [vm((2, 2 * levels, 128), F32) for _ in range(4)]
    scratch += [
        vm((spots, slots), BF16),
        vm((slots, 128), F32),
        vm((n_lat // 2, 2 * levels, 128), F32),
        vm((4 * levels, spots), BF16),
        vm((columns, spots), BF16),
        vm((2, TILES, levels, 128), F32),
        vm((2, TILES, levels, 128), F32),
        vm((TILES, 9, levels, 128), F32),
        vm((classes // 2 * levels, 6 * levels), BF16),
        vm((2, TILES, levels, 128), F32),
        vm((4 * levels, columns), BF16),
        vm((2 * MSG, spots), BF16),
        dma((9,)),
        dma((2,)),
    ]
    scratch += [dma((2, n_lev)) for _ in range(4)]
    scratch += [dma((n_lat,)) for _ in range(4)]
    scratch += [dma((4,)) for _ in range(4)]
    any_space = pl.BlockSpec(memory_space=pl.ANY)
    out, sens = pl.pallas_call(
        functools.partial(kernel, n_lev, n_lat),
        out_shape=(
            jax.ShapeDtypeStruct(adjoint_in.shape, F32),
            jax.ShapeDtypeStruct((slots, 2), F32),
        ),
        in_specs=[any_space] * len(operands),
        out_specs=(any_space, any_space),
        scratch_shapes=scratch,
        compiler_params=pltpu.CompilerParams(
            collective_id=0, has_side_effects=True, vmem_limit_bytes=40 * 2**20
        ),
    )(*operands)
    return out, sens.reshape(1, 1, slots, 2)


def solution(mesh):
    placed = (
        P(None, "lev", "lat", None),
        P(None, None, "lat", "lev"),
        P("lat", "lev"),
        P(),
        P("lev", "lat", None, None),
        P("lev", "lat", None, None),
        P("lev", "lat", None),
        P("lev", "lat", None),
        P("lev", "lat"),
    )
    return jax.shard_map(
        functools.partial(per_device, mesh.shape["lev"], mesh.shape["lat"]),
        mesh=mesh,
        in_specs=placed,
        out_specs=(P(None, "lev", "lat", None), P("lev", "lat", None, None)),
        check_vma=False,
    )
```

time: 187 us -> 65.3 us (0.35)
  the two profiles are of different devices: /device:TPU:1 before, /device:TPU:16 now
where the time goes in v1:
time: 65.3 us; the launch traced here: 65 us
  Pallas kernels  58.4 us (89%)
  local copies, waits for them, and re-layouts  5.19 us (8%)
  between operations  1.43 us (2%)
    pallas_call x1, Pallas kernels, per_device(): pl.pallas_call(functools.partial(kernel, n_lev, n_lat), out_shape=(jax.Sh...  58.4 us
    unnamed x16, local copies, waits for them, and re-layouts  5.19 us

profile of v1, /device:TPU:16, one launch (start us, length us, event | category | flops | bytes accessed | tf_op | source)
XLA Modules:
  0.0 65.0 jit_solution(15547322031442121300)
XLA Ops:
  0.6 0.0 copy-start
  1.3 1.0 %copy.11 = f32[1,1,512,64]{3,2,1,0:T(8,128)S(1)} copy(f32[1,1,512,64]{2,3,1,0:T(8,128)} %param.13) | data formatting | bytes 262144 | tf_op args[4]
  2.4 0.0 copy-start.3
  2.4 0.0 copy-start.4
  2.4 0.0 copy-start.5
  2.4 0.8 %copy.12 = f32[1,1,512,2]{3,2,1,0:T(8,128)S(1)} copy(f32[1,1,512,2]{2,3,1,0:T(2,128)} %param.14) | data formatting | bytes 8192 | tf_op args[5]
  3.3 0.0 copy-done
  3.3 0.0 copy-done.3
  3.3 0.0 copy-done.4
  3.3 0.0 copy-done.5
  3.3 0.0 copy-start.1
  3.3 0.9 %copy-done.1 = f32[2,2,16,1024]{3,2,1,0:T(8,128)S(1)} copy-done((f32[2,2,16,1024]{3,2,1,0:T(8,128)S(1)}, f32[2,2,16,1024]{3,2,1,0:T(8,128)}, u32[]{:S(2)}) %copy-start.1) | copy-done | bytes 262168
  4.3 0.0 copy-start.2
  4.3 0.9 %copy-done.2 = f32[16,32,32]{2,1,0:T(8,128)S(1)} copy-done((f32[16,32,32]{2,1,0:T(8,128)S(1)}, f32[16,32,32]{2,1,0:T(8,128)}, u32[]{:S(2)}) %copy-start.2) | copy-done | bytes 65560
  5.2 58.4 %shard_map.104 = (f32[2,2,16,1024]{3,2,1,0:T(8,128)S(1)}, f32[512,2]{1,0:T(8,128)S(1)}) custom-call(f32[2,2,16,1024]{3,2,1,0:T(8,128)S(1)} %copy-done.1, f32[2,512,64]{2,1,0:T(8,128)S(1)} %bitcast.8, s32[16,64]{1,0:T(8,128)S(1)} %copy-done.3, f32[16,32,32]{2,1,0:T(8,128)S(1)} %copy-done.2, f32[512,64]{1,0:T(8,128)S(1)} %bitcast.6, f32[512,2]{1,0:T(8,128)S(1)} %bitcast.7, ...), custom_call_target="tpu_custom_call" | custom-call | tf_op jit(solution)/shard_map/pallas_call | solution.py:614
  63.6 0.7 %copy.13 = f32[1,1,512,2]{2,3,1,0:T(2,128)} copy(f32[1,1,512,2]{3,2,1,0:T(8,128)S(1)} %bitcast.9) | data formatting | bytes 8192
  64.3 0.7 %copy.16 = f32[2,2,16,1024]{3,2,1,0:T(8,128)} copy(f32[2,2,16,1024]{3,2,1,0:T(8,128)S(1)} %get-tuple-element.10) | data formatting | bytes 524288
Async XLA Ops:
  0.6 2.6 %copy-start = (f32[2,32,16,64]{3,2,1,0:T(8,128)S(1)}, f32[2,32,16,64]{3,2,1,0:T(8,128)}, u32[]{:S(2)}) copy-start(f32[2,32,16,64]{3,2,1,0:T(8,128)} %param.10) | copy-start | bytes 786436
  2.4 0.9 %copy-start.3 = (s32[16,64]{1,0:T(8,128)S(1)}, s32[16,64]{1,0:T(8,128)}, u32[]{:S(2)}) copy-start(s32[16,64]{1,0:T(8,128)} %top_hbm.1) | copy-start | bytes 12292
  2.4 0.9 %copy-start.4 = (s32[1,1,512]{2,1,0:T(1,128)S(1)}, s32[1,1,512]{2,1,0:T(1,128)}, u32[]{:S(2)}) copy-start(s32[1,1,512]{2,1,0:T(1,128)} %param.15) | copy-start | bytes 6148
  2.4 0.9 %copy-start.5 = (s32[1,1,512]{2,1,0:T(1,128)S(1)}, s32[1,1,512]{2,1,0:T(1,128)}, u32[]{:S(2)}) copy-start(s32[1,1,512]{2,1,0:T(1,128)} %param.16) | copy-start | bytes 6148
  3.3 1.0 %copy-start.1 = (f32[2,2,16,1024]{3,2,1,0:T(8,128)S(1)}, f32[2,2,16,1024]{3,2,1,0:T(8,128)}, u32[]{:S(2)}) copy-start(f32[2,2,16,1024]{3,2,1,0:T(8,128)} %adj_hbm.1) | copy-start | bytes 786436
  4.3 0.9 %copy-start.2 = (f32[16,32,32]{2,1,0:T(8,128)S(1)}, f32[16,32,32]{2,1,0:T(8,128)}, u32[]{:S(2)}) copy-start(f32[16,32,32]{2,1,0:T(8,128)} %mat_hbm.1) | copy-start | bytes 196612

commit v2 on v1

--- a/solution.py
+++ b/solution.py
@@ -119,8 +119,8 @@
     owner_hbm,
     cell_hbm,
     count_hbm,
-    out_hbm,
-    sens_hbm,
+    out_ref,
+    sens_ref,
     adj_in,
     cour_in,
     top_in,
@@ -130,8 +130,6 @@
     owner_in,
     cell_in,
     count_in,
-    out_vm,
-    sens_vm,
     fwd_out,
     fwd_in,
     back_out,
@@ -149,7 +147,6 @@
     a_lat_out,
     a_lat_in,
     place,
-    payload,
     kern_rows,
     weighted,
     hot,
@@ -161,7 +158,6 @@
     conv_split,
     ret_split,
     in_sem,
-    out_sem,
     fwd_send,
     fwd_recv,
     back_send,
@@ -227,6 +223,7 @@
                 fwd_out[t, pl.ds(m * 32 + 16 + kk * 8, 8), :] = b
     pl.semaphore_wait(barrier, n_lev + n_lat - 2)
 
+
     def block(i):
         return pl.ds(pl.multiple_of(i * 16, 16), 16)
 
@@ -251,6 +248,7 @@
     start_fwd(1)
     for t in range(2):
         fwd_in[t, block(lev), :] = fwd_out[t, block(lev), :]
+
 
     for i in range(1, 6):
         loads[i].wait()
@@ -263,15 +261,11 @@
     slot = jnp.where(valid, owner * HALF + rank, -1)
     row = cell // HALF
     packed = (row % TILES) * 128 + (row // TILES) * HALF + cell % HALF
-    payload[...] = jnp.zeros((slots, 128), F32)
-    payload[:, 0 : 2 * levels] = kern_in[...]
-    payload[:, HALF : HALF + 2] = wt_in[...]
-    turned = jnp.transpose(payload[...])
-    small = turned[HALF : HALF + MSG, :]
-    small = jnp.where(
-        lax.broadcasted_iota(I32, (MSG, slots), 0) == 2, (packed + 1).astype(F32), small
-    )
-    table = jnp.concatenate([turned[0 : 2 * levels, :], small], axis=0)
+    which = lax.broadcasted_iota(I32, (MSG, slots), 0)
+    small = jnp.where(which == 2, (packed + 1).astype(F32), 0.0)
+    for t in range(2):
+        small = jnp.where(which == t, wt_in[t : t + 1, :], small)
+    table = jnp.concatenate([kern_in[...], small], axis=0)
     tall = 2 * levels + MSG
     table = jnp.concatenate(split(table), axis=0)
 
@@ -308,8 +302,10 @@
         msg_copy(d).start()
         return _
 
+
     lax.fori_loop(1, n_lat, start_msg, 0)
     msg_in[lat] = msg_out[lat]
+
 
     loads[6].wait()
     for c in range(2):
@@ -350,6 +346,7 @@
     for copy in c_copies:
         copy.start()
 
+
     loads[7].wait()
     loads[8].wait()
     for g in range(mat_in.shape[0] // 2):
@@ -380,11 +377,13 @@
             weights[p, 1 + i] = lon_w[j]
             weights[p, 5 + i] = lat_w[j]
 
+
     def wait_msg(d, _):
         msg_copy(d).wait()
         return _
 
     lax.fori_loop(1, n_lat, wait_msg, 0)
+
     columns = TILES * 128
 
     def arrive(m, _):
@@ -412,6 +411,7 @@
                     t * levels : (t + 1) * levels, i * 128 : (i + 1) * 128
                 ]
 
+
     def wait_fwd(t):
         def step(d, _):
             fwd_copy(t, d).wait()
@@ -419,6 +419,7 @@
 
         lax.fori_loop(1, n_lev, step, 0)
 
+    a_copies = []
     for t in range(2):
         wait_fwd(t)
         for q in range(TILES // 2):
@@ -444,14 +445,21 @@
             conv[t, 2 * q] = result[:, :128]
             conv[t, 2 * q + 1] = result[:, 128:]
         tiles = [conv[t, p] for p in range(TILES)]
-        rows_t = pl.ds(t * levels, levels)
-        a_lon_out[0, rows_t, :], a_lon_out[1, rows_t, :] = pack_lon(tiles)
-        a_lat_out[0, rows_t, :], a_lat_out[1, rows_t, :] = pack_lat(tiles)
-    a_copies = edge_copies(a_lon_out, a_lon_in, a_lat_out, a_lat_in, a_send, a_recv)
-    for copy in a_copies:
-        copy.start()
-    for copy in a_copies:
-        copy.wait()
+        a_lon_out[t, 0], a_lon_out[t, 1] = pack_lon(tiles)
+        a_lat_out[t, 0], a_lat_out[t, 1] = pack_lat(tiles)
+        a_copies.append(
+            edge_copies(
+                a_lon_out.at[t],
+                a_lon_in.at[t],
+                a_lat_out.at[t],
+                a_lat_in.at[t],
+                a_send.at[t],
+                a_recv.at[t],
+            )
+        )
+        for copy in a_copies[t]:
+            copy.start()
+
 
     def back_copy(t, d):
         return pltpu.make_async_remote_copy(
@@ -464,9 +472,10 @@
         )
 
     for t in range(2):
-        rows_t = pl.ds(t * levels, levels)
-        from_east, from_west = a_lon_in[0, rows_t, :], a_lon_in[1, rows_t, :]
-        from_north, from_south = a_lat_in[0, rows_t, :], a_lat_in[1, rows_t, :]
+        for copy in a_copies[t]:
+            copy.wait()
+        from_east, from_west = a_lon_in[t, 0], a_lon_in[t, 1]
+        from_north, from_south = a_lat_in[t, 0], a_lat_in[t, 1]
         from_north = jnp.where(last, 0.0, from_north)
         from_south = jnp.where(first, 0.0, from_south)
         tiles = extend_lat([conv[t, p] for p in range(TILES)], from_south, from_north)
@@ -485,6 +494,7 @@
 
         lax.fori_loop(1, n_lev, start_back, 0)
         back_in[t, block(lev), :] = back_out[t, block(lev), :]
+
 
     for m in range(n_lat // 4):
         picked = dot(conv_split[...], hot[:, pl.ds(m * 256, 256)])
@@ -518,17 +528,18 @@
         ret_copy(d).wait()
         return _
 
+
     lax.fori_loop(1, n_lat, start_ret, 0)
     ret_in[lat] = ret_out[lat]
     lax.fori_loop(1, n_lat, wait_ret, 0)
+
     for m in range(n_lat // 2):
         both, _unused = pair(ret_in[2 * m], ret_in[2 * m + 1])
         ret_split[:, pl.ds(m * 128, 128)] = jnp.concatenate(split(both), axis=0)
     own = dot(ret_split[...], place[...])
     own = own[:MSG] + own[MSG:]
-    sens_vm[...] = jnp.transpose(own)[:, 0:2]
-    sens_store = pltpu.make_async_copy(sens_vm, sens_hbm, out_sem.at[0])
-    sens_store.start()
+    sens_ref[...] = own[0:2]
+
 
     for t in range(2):
 
@@ -543,12 +554,8 @@
                     back_in[t, pl.ds(m * 32 + kk * 8, 8), :],
                     back_in[t, pl.ds(m * 32 + 16 + kk * 8, 8), :],
                 )
-                out_vm[t, kk, 0:8, pl.ds(m * 128, 128)] = a
-                out_vm[t, kk, 8:16, pl.ds(m * 128, 128)] = b
-    out_store = pltpu.make_async_copy(out_vm, out_hbm, out_sem.at[1])
-    out_store.start()
-    out_store.wait()
-    sens_store.wait()
+                out_ref[t, kk, 0:8, pl.ds(m * 128, 128)] = a
+                out_ref[t, kk, 8:16, pl.ds(m * 128, 128)] = b
 
 
 def per_device(
@@ -574,26 +581,21 @@
         courant.reshape(2, levels * ROWS, HALF),
         cloud_top,
         conv_inverse,
-        sounding_kernel.reshape(slots, 2 * levels),
-        sounding_weight.reshape(slots, 2),
+        sounding_kernel.reshape(slots, 2 * levels).T,
+        sounding_weight.reshape(slots, 2).T,
         sounding_owner.reshape(1, slots),
         sounding_cell.reshape(1, slots),
         sounding_count,
     )
     vm, dma = pltpu.VMEM, pltpu.SemaphoreType.DMA
     scratch = [vm(x.shape, x.dtype) for x in operands]
-    scratch += [
-        vm(adjoint_in.shape, F32),
-        vm((slots, 2), F32),
-    ]
     scratch += [vm((2, n_lev * 16, 128), F32) for _ in range(4)]
     scratch += [vm((n_lat, levels + MSG, 128), F32) for _ in range(2)]
     scratch += [vm((n_lat, MSG, 128), F32) for _ in range(2)]
     scratch += [vm((2, levels, 128), F32) for _ in range(4)]
-    scratch += [vm((2, 2 * levels, 128), F32) for _ in range(4)]
+    scratch += [vm((2, 2, levels, 128), F32) for _ in range(4)]
     scratch += [
         vm((spots, slots), BF16),
-        vm((slots, 128), F32),
         vm((n_lat // 2, 2 * levels, 128), F32),
         vm((4 * levels, spots), BF16),
         vm((columns, spots), BF16),
@@ -605,26 +607,27 @@
         vm((4 * levels, columns), BF16),
         vm((2 * MSG, spots), BF16),
         dma((9,)),
-        dma((2,)),
     ]
     scratch += [dma((2, n_lev)) for _ in range(4)]
     scratch += [dma((n_lat,)) for _ in range(4)]
-    scratch += [dma((4,)) for _ in range(4)]
-    any_space = pl.BlockSpec(memory_space=pl.ANY)
+    scratch += [dma((4,)) for _ in range(2)]
+    scratch += [dma((2, 4)) for _ in range(2)]
+    in_hbm = pl.BlockSpec(memory_space=pltpu.HBM)
+    in_vmem = pl.BlockSpec(memory_space=pltpu.VMEM)
     out, sens = pl.pallas_call(
         functools.partial(kernel, n_lev, n_lat),
         out_shape=(
             jax.ShapeDtypeStruct(adjoint_in.shape, F32),
-            jax.ShapeDtypeStruct((slots, 2), F32),
+            jax.ShapeDtypeStruct((2, slots), F32),
         ),
-        in_specs=[any_space] * len(operands),
-        out_specs=(any_space, any_space),
+        in_specs=[in_hbm] * len(operands),
+        out_specs=(in_vmem, in_vmem),
         scratch_shapes=scratch,
         compiler_params=pltpu.CompilerParams(
             collective_id=0, has_side_effects=True, vmem_limit_bytes=40 * 2**20
         ),
     )(*operands)
-    return out, sens.reshape(1, 1, slots, 2)
+    return out, sens.T.reshape(1, 1, slots, 2)
 
 
 def solution(mesh):

time: 65.3 us -> 67.1 us (1.028)
  local copies, waits for them, and re-layouts: 5.19 us -> 7.19 us
    unnamed x16 -> x18, local copies, waits for them, and re-layouts: 5.19 us -> 7.19 us
where the time goes in v2:
time: 67.1 us; the launch traced here: 66.8 us
  Pallas kernels  58.3 us (87%)
  local copies, waits for them, and re-layouts  7.19 us (11%)
  between operations  1.32 us (2%)
    pallas_call x1, Pallas kernels, per_device(): pl.pallas_call(functools.partial(kernel, n_lev, n_lat), out_shape=(jax.Sh...  58.3 us
    unnamed x18, local copies, waits for them, and re-layouts  7.19 us

profile of v2, /device:TPU:16, one launch (start us, length us, event | category | flops | bytes accessed | tf_op | source)
XLA Modules:
  0.0 66.8 jit_solution(12799640376846462239)
XLA Ops:
  0.6 0.0 copy-start.4
  1.3 0.0 copy-start.6
  1.3 0.0 copy-done.4
  1.3 0.7 copy-done.6
  2.0 0.0 copy-start
  2.0 1.0 %copy-done = f32[2,32,16,64]{3,2,1,0:T(8,128)S(1)} copy-done((f32[2,32,16,64]{3,2,1,0:T(8,128)S(1)}, f32[2,32,16,64]{3,2,1,0:T(8,128)}, u32[]{:S(2)}) %copy-start) | copy-done | bytes 262168
  3.0 0.0 copy-start.1
  3.0 0.9 %copy-done.1 = f32[2,2,16,1024]{3,2,1,0:T(8,128)S(1)} copy-done((f32[2,2,16,1024]{3,2,1,0:T(8,128)S(1)}, f32[2,2,16,1024]{3,2,1,0:T(8,128)}, u32[]{:S(2)}) %copy-start.1) | copy-done | bytes 262168
  4.0 0.0 copy-start.2
  4.0 0.9 %copy-done.2 = f32[16,32,32]{2,1,0:T(8,128)S(1)} copy-done((f32[16,32,32]{2,1,0:T(8,128)S(1)}, f32[16,32,32]{2,1,0:T(8,128)}, u32[]{:S(2)}) %copy-start.2) | copy-done | bytes 65560
  4.9 0.0 copy-start.3
  4.9 0.9 %copy-done.3 = f32[1,1,512,64]{2,3,1,0:T(8,128)S(1)} copy-done((f32[1,1,512,64]{2,3,1,0:T(8,128)S(1)}, f32[1,1,512,64]{2,3,1,0:T(8,128)}, u32[]{:S(2)}) %copy-start.3) | copy-done | bytes 131096
  5.8 0.0 copy-start.5
  5.8 0.7 %copy-done.5 = f32[1,1,512,2]{2,3,1,0:T(2,128)S(1)} copy-done((f32[1,1,512,2]{2,3,1,0:T(2,128)S(1)}, f32[1,1,512,2]{2,3,1,0:T(2,128)}, u32[]{:S(2)}) %copy-start.5) | copy-done | bytes 4120
  6.5 0.0 copy-start.7
  6.5 0.7 %copy-done.7 = s32[1,1,512]{2,1,0:T(1,128)S(1)} copy-done((s32[1,1,512]{2,1,0:T(1,128)S(1)}, s32[1,1,512]{2,1,0:T(1,128)}, u32[]{:S(2)}) %copy-start.7) | copy-done | bytes 2072
  7.2 58.3 %shard_map.104 = (f32[2,2,16,1024]{3,2,1,0:T(8,128)S(1)}, f32[2,512]{1,0:T(2,128)S(1)}) custom-call(f32[2,2,16,1024]{3,2,1,0:T(8,128)S(1)} %copy-done.1, f32[2,512,64]{2,1,0:T(8,128)S(1)} %bitcast.12, s32[16,64]{1,0:T(8,128)S(1)} %copy-done.4, f32[16,32,32]{2,1,0:T(8,128)S(1)} %copy-done.2, f32[64,512]{1,0:T(8,128)S(1)} %bitcast.13, f32[2,512]{1,0:T(2,128)S(1)} %bitcast.14, ...), custom_call_target="tpu_custom_call" | custom-call | tf_op jit(solution)/shard_map/pallas_call | solution.py:617
  65.5 0.7 %copy.14 = f32[2,2,16,1024]{3,2,1,0:T(8,128)} copy(f32[2,2,16,1024]{3,2,1,0:T(8,128)S(1)} %get-tuple-element.8) | data formatting | bytes 524288
  66.2 0.6 copy.15
Async XLA Ops:
  0.6 0.7 %copy-start.4 = (s32[16,64]{1,0:T(8,128)S(1)}, s32[16,64]{1,0:T(8,128)}, u32[]{:S(2)}) copy-start(s32[16,64]{1,0:T(8,128)} %top_hbm.1) | copy-start | bytes 12292
  1.3 0.7 %copy-start.6 = (s32[1,1,512]{2,1,0:T(1,128)S(1)}, s32[1,1,512]{2,1,0:T(1,128)}, u32[]{:S(2)}) copy-start(s32[1,1,512]{2,1,0:T(1,128)} %param.15) | copy-start | bytes 6148
  2.0 1.0 %copy-start = (f32[2,32,16,64]{3,2,1,0:T(8,128)S(1)}, f32[2,32,16,64]{3,2,1,0:T(8,128)}, u32[]{:S(2)}) copy-start(f32[2,32,16,64]{3,2,1,0:T(8,128)} %param.10) | copy-start | bytes 786436
  3.0 0.9 %copy-start.1 = (f32[2,2,16,1024]{3,2,1,0:T(8,128)S(1)}, f32[2,2,16,1024]{3,2,1,0:T(8,128)}, u32[]{:S(2)}) copy-start(f32[2,2,16,1024]{3,2,1,0:T(8,128)} %adj_hbm.1) | copy-start | bytes 786436
  4.0 0.9 %copy-start.2 = (f32[16,32,32]{2,1,0:T(8,128)S(1)}, f32[16,32,32]{2,1,0:T(8,128)}, u32[]{:S(2)}) copy-start(f32[16,32,32]{2,1,0:T(8,128)} %mat_hbm.1) | copy-start | bytes 196612
  4.9 0.9 %copy-start.3 = (f32[1,1,512,64]{2,3,1,0:T(8,128)S(1)}, f32[1,1,512,64]{2,3,1,0:T(8,128)}, u32[]{:S(2)}) copy-start(f32[1,1,512,64]{2,3,1,0:T(8,128)} %param.13) | copy-start | bytes 393220
  5.8 0.7 %copy-start.5 = (f32[1,1,512,2]{2,3,1,0:T(2,128)S(1)}, f32[1,1,512,2]{2,3,1,0:T(2,128)}, u32[]{:S(2)}) copy-start(f32[1,1,512,2]{2,3,1,0:T(2,128)} %param.14) | copy-start | bytes 12292
  6.5 0.7 %copy-start.7 = (s32[1,1,512]{2,1,0:T(1,128)S(1)}, s32[1,1,512]{2,1,0:T(1,128)}, u32[]{:S(2)}) copy-start(s32[1,1,512]{2,1,0:T(1,128)} %param.16) | copy-start | bytes 6148

commit v3 on v2

--- a/solution.py
+++ b/solution.py
@@ -181,6 +181,23 @@
     def lat_at(d):
         return lax.rem(lat + d + n_lat, n_lat)
 
+    n_y = max(2, n_lat // 8)
+    n_x = n_lat // (2 * n_y)
+    at_x, at_y, core = lat // (2 * n_y), lax.rem(lat // 2, n_y), lax.rem(lat, 2)
+
+    def hops(step):
+        return min(step[0], n_x - step[0]) + min(step[1], n_y - step[1])
+
+    chips = sorted(((i, j) for i in range(n_x) for j in range(n_y)), key=hops, reverse=True)
+
+    def chip_at(n, sign):
+        i, j = chips[n]
+        return lax.rem(at_x + sign * i + n_x, n_x) * n_y + lax.rem(at_y + sign * j + n_y, n_y)
+
+    def far(i):
+        half = (i + 1) // 2
+        return n_lev // 2 + half * (1 - 2 * lax.rem(i, 2))
+
     loads = [
         pltpu.make_async_copy(source, target, in_sem.at[i])
         for i, (source, target) in enumerate(
@@ -238,11 +255,11 @@
         )
 
     def start_fwd(t):
-        def step(d, _):
-            fwd_copy(t, d).start()
+        def step(i, _):
+            fwd_copy(t, far(i)).start()
             return _
 
-        lax.fori_loop(1, n_lev, step, 0)
+        lax.fori_loop(0, n_lev - 1, step, 0)
 
     start_fwd(0)
     start_fwd(1)
@@ -269,41 +286,39 @@
     tall = 2 * levels + MSG
     table = jnp.concatenate(split(table), axis=0)
 
-    def route(q, _):
-        base = pl.multiple_of(q * 256, 256)
-        spot = lax.broadcasted_iota(I32, (256, slots), 0) + base
+    def route(m):
+        base = pl.multiple_of(m * 128, 128)
+        spot = lax.broadcasted_iota(I32, (128, slots), 0) + base
         hits = one_hot(spot == slot)
-        place[pl.ds(base, 256), :] = hits
+        place[pl.ds(base, 128), :] = hits
         sent = dot(table, hits, (1, 1))
         sent = sent[:tall] + sent[tall:]
-        for m in range(2):
-            part = sent[:, m * 128 : (m + 1) * 128]
-            a, b = pair(part[:levels], part[levels : 2 * levels])
-            rest = part[2 * levels :]
-            msg_out[q * 4 + m * 2, 0:levels, :] = a
-            msg_out[q * 4 + m * 2 + 1, 0:levels, :] = b
-            msg_out[q * 4 + m * 2, levels : levels + MSG, :] = rest
-            msg_out[q * 4 + m * 2 + 1, levels : levels + MSG, :] = turn(rest, HALF)
-        return _
-
-    lax.fori_loop(0, n_lat // 4, route, 0)
-
-    def msg_copy(d):
+        a, b = pair(sent[:levels], sent[levels : 2 * levels])
+        rest = sent[2 * levels :]
+        msg_out[2 * m, 0:levels, :] = a
+        msg_out[2 * m + 1, 0:levels, :] = b
+        msg_out[2 * m, levels : levels + MSG, :] = rest
+        msg_out[2 * m + 1, levels : levels + MSG, :] = turn(rest, HALF)
+
+    def msg_copy(n, change):
+        target = 2 * chip_at(n, 1) + lax.rem(core + change, 2)
         return pltpu.make_async_remote_copy(
-            src_ref=msg_out.at[lat_at(d)],
+            src_ref=msg_out.at[target],
             dst_ref=msg_in.at[lat],
-            send_sem=msg_send.at[d],
-            recv_sem=msg_recv.at[d],
-            device_id={"lat": lat_at(d)},
+            send_sem=msg_send.at[2 * n + change],
+            recv_sem=msg_recv.at[2 * n + change],
+            device_id={"lat": target},
             device_id_type=MESH,
         )
 
-    def start_msg(d, _):
-        msg_copy(d).start()
-        return _
-
-
-    lax.fori_loop(1, n_lat, start_msg, 0)
+    def others(n):
+        return (1,) if chips[n] == (0, 0) else (0, 1)
+
+
+    for n in range(len(chips)):
+        route(chip_at(n, 1))
+        for change in others(n):
+            msg_copy(n, change).start()
     msg_in[lat] = msg_out[lat]
 
 
@@ -378,39 +393,39 @@
             weights[p, 5 + i] = lat_w[j]
 
 
-    def wait_msg(d, _):
-        msg_copy(d).wait()
-        return _
-
-    lax.fori_loop(1, n_lat, wait_msg, 0)
-
     columns = TILES * 128
 
-    def arrive(m, _):
+    def arrive(n):
+        m = chip_at(n, -1)
         a, b = msg_in[2 * m], msg_in[2 * m + 1]
         one, two = pair(a[:levels], b[:levels])
         rest, _unused = pair(a[levels:], b[levels:])
-        kern_rows[m, 0:levels, :] = one
-        kern_rows[m, levels : 2 * levels, :] = two
+        kern_rows[n, 0:levels, :] = one
+        kern_rows[n, levels : 2 * levels, :] = two
         wk = jnp.concatenate([one * rest[0:1], two * rest[1:2]], axis=0)
-        at = pl.ds(pl.multiple_of(m * 128, 128), 128)
+        at = pl.ds(n * 128, 128)
         high, low = split(wk)
         weighted[0 : 2 * levels, at] = high
         weighted[2 * levels :, at] = low
         target = rest[2:3].astype(I32) - 1
         hot[:, at] = one_hot(lax.broadcasted_iota(I32, (columns, 128), 0) == target)
-        return _
-
-    lax.fori_loop(0, n_lat // 2, arrive, 0)
-    for q in range(TILES // 2):
-        got = dot(weighted[...], hot[pl.ds(q * 256, 256), :], (1, 1))
-        got = got[: 2 * levels] + got[2 * levels :]
-        for t in range(2):
-            for i in range(2):
-                deposit[t, 2 * q + i] = got[
-                    t * levels : (t + 1) * levels, i * 128 : (i + 1) * 128
-                ]
-
+
+    group = max(1, len(chips) // 4)
+    for g in range(len(chips) // group):
+        for n in range(g * group, (g + 1) * group):
+            for change in others(n):
+                msg_copy(n, change).wait()
+            arrive(n)
+        taken = pl.ds(g * group * 128, group * 128)
+        for q in range(TILES // 2):
+            got = dot(weighted[:, taken], hot[pl.ds(q * 256, 256), taken], (1, 1))
+            got = got[: 2 * levels] + got[2 * levels :]
+            for t in range(2):
+                for i in range(2):
+                    part = got[t * levels : (t + 1) * levels, i * 128 : (i + 1) * 128]
+                    if g > 0:
+                        part = part + deposit[t, 2 * q + i]
+                    deposit[t, 2 * q + i] = part
 
     def wait_fwd(t):
         def step(d, _):
@@ -488,11 +503,11 @@
                 total = total + weights[p, 1 + i] * around[i]
             back_out[t, pl.ds(p, levels, stride=TILES), :] = total
 
-        def start_back(d, _, t=t):
-            back_copy(t, d).start()
+        def start_back(i, _, t=t):
+            back_copy(t, far(i)).start()
             return _
 
-        lax.fori_loop(1, n_lev, start_back, 0)
+        lax.fori_loop(0, n_lev - 1, start_back, 0)
         back_in[t, block(lev), :] = back_out[t, block(lev), :]
 
 
@@ -510,28 +525,25 @@
             ret_out[4 * m + 2 * i] = both
             ret_out[4 * m + 2 * i + 1] = turn(both, HALF)
 
-    def ret_copy(d):
+    def ret_copy(n, change):
+        other = lax.rem(core + change, 2)
         return pltpu.make_async_remote_copy(
-            src_ref=ret_out.at[lat_at(d)],
+            src_ref=ret_out.at[2 * n + other],
             dst_ref=ret_in.at[lat],
-            send_sem=ret_send.at[d],
-            recv_sem=ret_recv.at[d],
-            device_id={"lat": lat_at(d)},
+            send_sem=ret_send.at[2 * n + change],
+            recv_sem=ret_recv.at[2 * n + change],
+            device_id={"lat": 2 * chip_at(n, -1) + other},
             device_id_type=MESH,
         )
 
-    def start_ret(d, _):
-        ret_copy(d).start()
-        return _
-
-    def wait_ret(d, _):
-        ret_copy(d).wait()
-        return _
-
-
-    lax.fori_loop(1, n_lat, start_ret, 0)
-    ret_in[lat] = ret_out[lat]
-    lax.fori_loop(1, n_lat, wait_ret, 0)
+
+    for n in range(len(chips)):
+        for change in others(n):
+            ret_copy(n, change).start()
+    ret_in[lat] = ret_out[n_lat - 2 + core]
+    for n in range(len(chips)):
+        for change in others(n):
+            ret_copy(n, change).wait()
 
     for m in range(n_lat // 2):
         both, _unused = pair(ret_in[2 * m], ret_in[2 * m + 1])
@@ -624,7 +636,7 @@
         out_specs=(in_vmem, in_vmem),
         scratch_shapes=scratch,
         compiler_params=pltpu.CompilerParams(
-            collective_id=0, has_side_effects=True, vmem_limit_bytes=40 * 2**20
+            collective_id=0, has_side_effects=True, vmem_limit_bytes=60 * 2**20
         ),
     )(*operands)
     return out, sens.T.reshape(1, 1, slots, 2)

time: 67.1 us -> 58.7 us (0.87)
  the two profiles are of different devices: /device:TPU:16 before, /device:TPU:1 now
where the time goes in v3:
time: 58.7 us; the launch traced here: 57.6 us
  Pallas kernels  54 us (92%)
  local copies, waits for them, and re-layouts  2.27 us (4%)
  between operations  1.3 us (2%)
    pallas_call x1, Pallas kernels, per_device(): pl.pallas_call(functools.partial(kernel, n_lev, n_lat), out_shape=(jax.Sh...  54 us
    unnamed x4, local copies, waits for them, and re-layouts  2.27 us

profile of v3, /device:TPU:1, one launch (start us, length us, event | category | flops | bytes accessed | tf_op | source)
XLA Modules:
  0.0 57.6 jit_solution(272515492704147645)
XLA Ops:
  1.3 54.0 %shard_map.104 = (f32[2,2,16,1024]{3,2,1,0:T(8,128)}, f32[2,512]{1,0:T(2,128)}) custom-call(f32[2,2,16,1024]{3,2,1,0:T(8,128)} %adj_hbm.1, f32[2,512,64]{2,1,0:T(8,128)} %bitcast.12, s32[16,64]{1,0:T(8,128)} %top_hbm.1, f32[16,32,32]{2,1,0:T(8,128)} %mat_hbm.1, f32[64,512]{1,0:T(8,128)} %bitcast.13, f32[2,512]{1,0:T(2,128)} %bitcast.14, s32[1,512]{1,0:T(1,128)} %bitcast.16, ...), custom_call_target="tpu_custom_call" | custom-call | tf_op jit(solution)/shard_map/pallas_call | solution.py:629
  55.3 0.0 copy-start
  55.3 1.7 %copy.14 = f32[2,2,16,1024]{3,2,1,0:T(8,128)} copy(f32[2,2,16,1024]{3,2,1,0:T(8,128)} %get-tuple-element.8) | data formatting | bytes 524288
  57.0 0.0 copy-done
  57.0 0.6 %copy.15 = f32[1,1,512,2]{2,3,1,0:T(2,128)} copy(f32[1,1,512,2]{2,3,1,0:T(2,128)S(1)} %bitcast.15) | data formatting | bytes 8192
Async XLA Ops:
  55.3 1.7 %copy-start = (f32[2,512]{1,0:T(2,128)S(1)}, f32[2,512]{1,0:T(2,128)}, u32[]{:S(2)}) copy-start(f32[2,512]{1,0:T(2,128)} %get-tuple-element.5) | copy-start | bytes 12292

commit v4 on v3

--- a/solution.py
+++ b/solution.py
@@ -12,6 +12,8 @@
 ROWS = 16
 TILES = 8
 HALF = 64
+USED = 48
+SMALL = 8
 MSG = 8
 
 
@@ -119,7 +121,7 @@
     owner_hbm,
     cell_hbm,
     count_hbm,
-    out_ref,
+    back_in,
     sens_ref,
     adj_in,
     cour_in,
@@ -133,7 +135,6 @@
     fwd_out,
     fwd_in,
     back_out,
-    back_in,
     msg_out,
     msg_in,
     ret_out,
@@ -158,6 +159,7 @@
     conv_split,
     ret_split,
     in_sem,
+    keep_sem,
     fwd_send,
     fwd_recv,
     back_send,
@@ -278,27 +280,38 @@
     slot = jnp.where(valid, owner * HALF + rank, -1)
     row = cell // HALF
     packed = (row % TILES) * 128 + (row // TILES) * HALF + cell % HALF
-    which = lax.broadcasted_iota(I32, (MSG, slots), 0)
-    small = jnp.where(which == 2, (packed + 1).astype(F32), 0.0)
-    for t in range(2):
-        small = jnp.where(which == t, wt_in[t : t + 1, :], small)
+    which = lax.broadcasted_iota(I32, (2 * SMALL, slots), 0)
+    small = jnp.where((which >= 3) & (which < 6), (packed + 1).astype(F32), 0.0)
+    small = jnp.where(which < 3, wt_in[0:1, :], small)
+    small = jnp.where((which >= SMALL) & (which < SMALL + 3), wt_in[1:2, :], small)
     table = jnp.concatenate([kern_in[...], small], axis=0)
-    tall = 2 * levels + MSG
+    tall = 2 * levels + 2 * SMALL
     table = jnp.concatenate(split(table), axis=0)
 
-    def route(m):
-        base = pl.multiple_of(m * 128, 128)
-        spot = lax.broadcasted_iota(I32, (128, slots), 0) + base
-        hits = one_hot(spot == slot)
-        place[pl.ds(base, 128), :] = hits
-        sent = dot(table, hits, (1, 1))
+    def route(chips_m):
+        hits = []
+        for m in chips_m:
+            base = pl.multiple_of(m * 128, 128)
+            spot = lax.broadcasted_iota(I32, (128, slots), 0) + base
+            hits.append(one_hot(spot == slot))
+            place[pl.ds(base, 128), :] = hits[-1]
+        sent = dot(table, jnp.concatenate(hits, axis=0), (1, 1))
         sent = sent[:tall] + sent[tall:]
-        a, b = pair(sent[:levels], sent[levels : 2 * levels])
-        rest = sent[2 * levels :]
-        msg_out[2 * m, 0:levels, :] = a
-        msg_out[2 * m + 1, 0:levels, :] = b
-        msg_out[2 * m, levels : levels + MSG, :] = rest
-        msg_out[2 * m + 1, levels : levels + MSG, :] = turn(rest, HALF)
+        for i, m in enumerate(chips_m):
+            part = sent[:, i * 128 : (i + 1) * 128]
+            t0 = jnp.concatenate([part[:levels], part[2 * levels : 2 * levels + SMALL]], axis=0)
+            t1 = jnp.concatenate(
+                [part[levels : 2 * levels], part[2 * levels + SMALL :]], axis=0
+            )
+            for change, full in enumerate(pair(t0, t1)):
+                rest = full[levels:]
+                third = lax.broadcasted_iota(I32, rest.shape, 0) % 3
+                moved = jnp.where(third == 1, turn(rest, 32), turn(rest, 16))
+                moved = jnp.where(third == 0, turn(rest, 48), moved)
+                free = lanes(rest.shape) % HALF >= USED
+                msg_out[2 * m + change, 0:SMALL, :] = jnp.where(free, moved, full[:SMALL])
+                if levels > SMALL:
+                    msg_out[2 * m + change, SMALL:levels, :] = full[SMALL:levels]
 
     def msg_copy(n, change):
         target = 2 * chip_at(n, 1) + lax.rem(core + change, 2)
@@ -315,10 +328,12 @@
         return (1,) if chips[n] == (0, 0) else (0, 1)
 
 
-    for n in range(len(chips)):
-        route(chip_at(n, 1))
-        for change in others(n):
-            msg_copy(n, change).start()
+    group = max(1, len(chips) // 4)
+    for g in range(0, len(chips), group):
+        route([chip_at(n, 1) for n in range(g, g + group)])
+        for n in range(g, g + group):
+            for change in others(n):
+                msg_copy(n, change).start()
     msg_in[lat] = msg_out[lat]
 
 
@@ -372,45 +387,31 @@
         mix[pl.ds(g * levels, levels), :] = jnp.concatenate(wide, axis=1)
     tops = jnp.concatenate([top_in[0:8, :], top_in[8:16, :]], axis=1)
 
-    first, last = lat == 0, lat == n_lat - 1
-    for copy in c_copies:
-        copy.wait()
-    from_east, from_west = c_lon_in[0], c_lon_in[1]
-    from_north, from_south = c_lat_in[0], c_lat_in[1]
-    from_north = jnp.where(last, 0.0, from_north)
-    from_south = jnp.where(first, 0.0, from_south)
-    rows_c = [cour_t[1, p] for p in range(TILES)]
-    rows_c[0] = jnp.where(low_half(rows_c[0].shape) & first, 0.0, rows_c[0])
-    rows_c = extend_lat(rows_c, from_south, from_north)
-    for p in range(TILES):
-        here = cour_t[0, p]
-        before_x, after_x, after2_x = shift_lon(here, p, from_west, from_east, (-1, 1, 2))
-        lon_w = face_weights(before_x, here, after_x, after2_x)
-        lat_w = face_weights(rows_c[p + 1], rows_c[p + 2], rows_c[p + 3], rows_c[p + 4])
-        weights[p, 0] = 1.0 + lon_w[2] + lat_w[2]
-        for i, j in enumerate((0, 1, 3, 4)):
-            weights[p, 1 + i] = lon_w[j]
-            weights[p, 5 + i] = lat_w[j]
-
 
     columns = TILES * 128
 
     def arrive(n):
         m = chip_at(n, -1)
-        a, b = msg_in[2 * m], msg_in[2 * m + 1]
-        one, two = pair(a[:levels], b[:levels])
-        rest, _unused = pair(a[levels:], b[levels:])
+        one, two = pair(msg_in[2 * m], msg_in[2 * m + 1])
         kern_rows[n, 0:levels, :] = one
         kern_rows[n, levels : 2 * levels, :] = two
-        wk = jnp.concatenate([one * rest[0:1], two * rest[1:2]], axis=0)
+
+        def small_row(rows, first):
+            third = lanes((1, 128)) % HALF // 16
+            out = jnp.zeros((1, 128), F32)
+            for i in range(3):
+                moved = turn(rows[:SMALL], 16 * i - USED)
+                out = jnp.where(third == i, moved[first + i : first + i + 1], out)
+            return out
+
+        wk = jnp.concatenate([one * small_row(one, 0), two * small_row(two, 0)], axis=0)
         at = pl.ds(n * 128, 128)
         high, low = split(wk)
         weighted[0 : 2 * levels, at] = high
         weighted[2 * levels :, at] = low
-        target = rest[2:3].astype(I32) - 1
+        target = small_row(one, 3).astype(I32) - 1
         hot[:, at] = one_hot(lax.broadcasted_iota(I32, (columns, 128), 0) == target)
 
-    group = max(1, len(chips) // 4)
     for g in range(len(chips) // group):
         for n in range(g * group, (g + 1) * group):
             for change in others(n):
@@ -426,6 +427,7 @@
                     if g > 0:
                         part = part + deposit[t, 2 * q + i]
                     deposit[t, 2 * q + i] = part
+
 
     def wait_fwd(t):
         def step(d, _):
@@ -475,6 +477,26 @@
         for copy in a_copies[t]:
             copy.start()
 
+    first, last = lat == 0, lat == n_lat - 1
+    for copy in c_copies:
+        copy.wait()
+    from_east, from_west = c_lon_in[0], c_lon_in[1]
+    from_north, from_south = c_lat_in[0], c_lat_in[1]
+    from_north = jnp.where(last, 0.0, from_north)
+    from_south = jnp.where(first, 0.0, from_south)
+    rows_c = [cour_t[1, p] for p in range(TILES)]
+    rows_c[0] = jnp.where(low_half(rows_c[0].shape) & first, 0.0, rows_c[0])
+    rows_c = extend_lat(rows_c, from_south, from_north)
+    for p in range(TILES):
+        here = cour_t[0, p]
+        before_x, after_x, after2_x = shift_lon(here, p, from_west, from_east, (-1, 1, 2))
+        lon_w = face_weights(before_x, here, after_x, after2_x)
+        lat_w = face_weights(rows_c[p + 1], rows_c[p + 2], rows_c[p + 3], rows_c[p + 4])
+        weights[p, 0] = 1.0 + lon_w[2] + lat_w[2]
+        for i, j in enumerate((0, 1, 3, 4)):
+            weights[p, 1 + i] = lon_w[j]
+            weights[p, 5 + i] = lat_w[j]
+
 
     def back_copy(t, d):
         return pltpu.make_async_remote_copy(
@@ -486,6 +508,7 @@
             device_id_type=MESH,
         )
 
+    keeps = []
     for t in range(2):
         for copy in a_copies[t]:
             copy.wait()
@@ -508,7 +531,12 @@
             return _
 
         lax.fori_loop(0, n_lev - 1, start_back, 0)
-        back_in[t, block(lev), :] = back_out[t, block(lev), :]
+        keeps.append(
+            pltpu.make_async_copy(
+                back_out.at[t, block(lev), :], back_in.at[t, block(lev), :], keep_sem.at[t]
+            )
+        )
+        keeps[t].start()
 
 
     for m in range(n_lat // 4):
@@ -560,14 +588,31 @@
             return _
 
         lax.fori_loop(1, n_lev, wait_back, 0)
+        keeps[t].wait()
+
+
+def finish(n_lev, back_hbm, sens_hbm, out_hbm, sens_out, back, out, load_sem, store_sem):
+    loads, stores = [], []
+    for t in range(2):
+        loads.append(pltpu.make_async_copy(back_hbm.at[t], back.at[t], load_sem.at[t]))
+        loads[t].start()
+        stores.append(pltpu.make_async_copy(out.at[t], out_hbm.at[t], store_sem.at[t]))
+    sens_copy = pltpu.make_async_copy(sens_hbm, sens_out, store_sem.at[2])
+    sens_copy.start()
+    for t in range(2):
+        loads[t].wait()
         for m in range(n_lev // 2):
             for kk in range(2):
                 a, b = pair(
-                    back_in[t, pl.ds(m * 32 + kk * 8, 8), :],
-                    back_in[t, pl.ds(m * 32 + 16 + kk * 8, 8), :],
+                    back[t, pl.ds(m * 32 + kk * 8, 8), :],
+                    back[t, pl.ds(m * 32 + 16 + kk * 8, 8), :],
                 )
-                out_ref[t, kk, 0:8, pl.ds(m * 128, 128)] = a
-                out_ref[t, kk, 8:16, pl.ds(m * 128, 128)] = b
+                out[t, kk, 0:8, pl.ds(m * 128, 128)] = a
+                out[t, kk, 8:16, pl.ds(m * 128, 128)] = b
+        stores[t].start()
+    for store in stores:
+        store.wait()
+    sens_copy.wait()
 
 
 def per_device(
@@ -601,8 +646,8 @@
     )
     vm, dma = pltpu.VMEM, pltpu.SemaphoreType.DMA
     scratch = [vm(x.shape, x.dtype) for x in operands]
-    scratch += [vm((2, n_lev * 16, 128), F32) for _ in range(4)]
-    scratch += [vm((n_lat, levels + MSG, 128), F32) for _ in range(2)]
+    scratch += [vm((2, n_lev * 16, 128), F32) for _ in range(3)]
+    scratch += [vm((n_lat, levels, 128), F32) for _ in range(2)]
     scratch += [vm((n_lat, MSG, 128), F32) for _ in range(2)]
     scratch += [vm((2, levels, 128), F32) for _ in range(4)]
     scratch += [vm((2, 2, levels, 128), F32) for _ in range(4)]
@@ -619,6 +664,7 @@
         vm((4 * levels, columns), BF16),
         vm((2 * MSG, spots), BF16),
         dma((9,)),
+        dma((2,)),
     ]
     scratch += [dma((2, n_lev)) for _ in range(4)]
     scratch += [dma((n_lat,)) for _ in range(4)]
@@ -626,19 +672,35 @@
     scratch += [dma((2, 4)) for _ in range(2)]
     in_hbm = pl.BlockSpec(memory_space=pltpu.HBM)
     in_vmem = pl.BlockSpec(memory_space=pltpu.VMEM)
-    out, sens = pl.pallas_call(
+    back, sens = pl.pallas_call(
         functools.partial(kernel, n_lev, n_lat),
         out_shape=(
-            jax.ShapeDtypeStruct(adjoint_in.shape, F32),
+            jax.ShapeDtypeStruct((2, n_lev * 16, 128), F32),
             jax.ShapeDtypeStruct((2, slots), F32),
         ),
         in_specs=[in_hbm] * len(operands),
-        out_specs=(in_vmem, in_vmem),
+        out_specs=(in_hbm, in_vmem),
         scratch_shapes=scratch,
         compiler_params=pltpu.CompilerParams(
             collective_id=0, has_side_effects=True, vmem_limit_bytes=60 * 2**20
         ),
     )(*operands)
+    out, sens = pl.pallas_call(
+        functools.partial(finish, n_lev),
+        out_shape=(
+            jax.ShapeDtypeStruct(adjoint_in.shape, F32),
+            jax.ShapeDtypeStruct((2, slots), F32),
+        ),
+        in_specs=[in_hbm] * 2,
+        out_specs=(in_hbm, in_hbm),
+        scratch_shapes=[
+            vm((2, n_lev * 16, 128), F32),
+            vm(adjoint_in.shape, F32),
+            dma((2,)),
+            dma((3,)),
+        ],
+        compiler_params=pltpu.CompilerParams(vmem_limit_bytes=60 * 2**20),
+    )(back, sens)
     return out, sens.T.reshape(1, 1, slots, 2)
 
 

time: 58.7 us -> 54.1 us (0.922); the launches traced: 57.6 us -> 54 us
  local copies, waits for them, and re-layouts: 2.27 us -> 0 us
  Pallas kernels: 54 us -> 52.7 us
    pallas_call x1, Pallas kernels: 54 us -> 50.9 us  [per_device(): pl.pallas_call(functools.partial(kernel, n_lev, n_lat), out_shape=(jax.Sh...]
    unnamed x4 -> x0, local copies, waits for them, and re-layouts: 2.27 us -> none
    pallas_call x0 -> x1, Pallas kernels: none -> 1.81 us  [per_device(): pl.pallas_call(functools.partial(finish, n_lev), out_shape=(jax.ShapeDtyp...]
where the time goes in v4:
time: 54.1 us; the launch traced here: 54 us
  Pallas kernels  52.7 us (97%)
  between operations  1.29 us (2%)
    pallas_call x1, Pallas kernels, per_device(): pl.pallas_call(functools.partial(kernel, n_lev, n_lat), out_shape=(jax.Sh...  50.9 us
    pallas_call x1, Pallas kernels, per_device(): pl.pallas_call(functools.partial(finish, n_lev), out_shape=(jax.ShapeDtyp...  1.81 us

profile of v4, /device:TPU:1, one launch (start us, length us, event | category | flops | bytes accessed | tf_op | source)
XLA Modules:
  0.0 54.0 jit_solution(15375029567650833308)
XLA Ops:
  1.3 50.9 %shard_map.104 = (f32[2,256,128]{2,1,0:T(8,128)}, f32[2,512]{1,0:T(2,128)}) custom-call(f32[2,2,16,1024]{3,2,1,0:T(8,128)} %adj_hbm.1, f32[2,512,64]{2,1,0:T(8,128)} %bitcast.12, s32[16,64]{1,0:T(8,128)} %top_hbm.1, f32[16,32,32]{2,1,0:T(8,128)} %mat_hbm.1, f32[64,512]{1,0:T(8,128)} %bitcast.13, f32[2,512]{1,0:T(2,128)} %bitcast.14, s32[1,512]{1,0:T(1,128)} %bitcast.15, ...), custom_call_target="tpu_custom_call" | custom-call | tf_op jit(solution)/shard_map/pallas_call | solution.py:675
  52.2 1.8 %shard_map.105 = (f32[2,2,16,1024]{3,2,1,0:T(8,128)}, f32[2,512]{1,0:T(2,128)}) custom-call(f32[2,256,128]{2,1,0:T(8,128)} %get-tuple-element.6.back_hbm, f32[2,512]{1,0:T(2,128)} %get-tuple-element.7.sens_hbm), custom_call_target="tpu_custom_call" | custom-call | tf_op jit(solution)/shard_map/pallas_call | solution.py:688

commit v5 on v4

--- a/solution.py
+++ b/solution.py
@@ -120,7 +120,7 @@
     wt_hbm,
     owner_hbm,
     cell_hbm,
-    count_hbm,
+    count_ref,
     back_in,
     sens_ref,
     adj_in,
@@ -131,7 +131,6 @@
     wt_in,
     owner_in,
     cell_in,
-    count_in,
     fwd_out,
     fwd_in,
     back_out,
@@ -190,7 +189,7 @@
     def hops(step):
         return min(step[0], n_x - step[0]) + min(step[1], n_y - step[1])
 
-    chips = sorted(((i, j) for i in range(n_x) for j in range(n_y)), key=hops, reverse=True)
+    chips = sorted(((i, j) for i in range(n_x) for j in range(n_y)), key=hops)
 
     def chip_at(n, sign):
         i, j = chips[n]
@@ -207,7 +206,6 @@
                 (adj_hbm, adj_in),
                 (owner_hbm, owner_in),
                 (cell_hbm, cell_in),
-                (count_hbm, count_in),
                 (kern_hbm, kern_in),
                 (wt_hbm, wt_in),
                 (cour_hbm, cour_in),
@@ -222,14 +220,14 @@
     barrier = pltpu.get_barrier_semaphore()
 
     def greet_lev(d, _):
-        pl.semaphore_signal(barrier, inc=1, device_id={"lev": lev_at(d)}, device_id_type=MESH)
+        pl.semaphore_signal(barrier, inc=1, device_id={"lev": lev_at(far(d))}, device_id_type=MESH)
         return _
 
     def greet_lat(d, _):
         pl.semaphore_signal(barrier, inc=1, device_id={"lat": lat_at(d)}, device_id_type=MESH)
         return _
 
-    lax.fori_loop(1, n_lev, greet_lev, 0)
+    lax.fori_loop(0, n_lev - 1, greet_lev, 0)
     lax.fori_loop(1, n_lat, greet_lat, 0)
 
     loads[0].wait()
@@ -240,39 +238,10 @@
                 a, b = pair(adj_in[t, kk, 0:8, cols], adj_in[t, kk, 8:16, cols])
                 fwd_out[t, pl.ds(m * 32 + kk * 8, 8), :] = a
                 fwd_out[t, pl.ds(m * 32 + 16 + kk * 8, 8), :] = b
-    pl.semaphore_wait(barrier, n_lev + n_lat - 2)
-
-
-    def block(i):
-        return pl.ds(pl.multiple_of(i * 16, 16), 16)
-
-    def fwd_copy(t, d):
-        return pltpu.make_async_remote_copy(
-            src_ref=fwd_out.at[t, block(lev_at(d)), :],
-            dst_ref=fwd_in.at[t, block(lev), :],
-            send_sem=fwd_send.at[t, d],
-            recv_sem=fwd_recv.at[t, d],
-            device_id={"lev": lev_at(d)},
-            device_id_type=MESH,
-        )
-
-    def start_fwd(t):
-        def step(i, _):
-            fwd_copy(t, far(i)).start()
-            return _
-
-        lax.fori_loop(0, n_lev - 1, step, 0)
-
-    start_fwd(0)
-    start_fwd(1)
-    for t in range(2):
-        fwd_in[t, block(lev), :] = fwd_out[t, block(lev), :]
-
-
-    for i in range(1, 6):
+    for i in range(1, 5):
         loads[i].wait()
     owner, cell = owner_in[...], cell_in[...]
-    valid = lanes((1, slots)) < count_in[...]
+    valid = lanes((1, slots)) < count_ref[0, 0]
     owned = (lax.broadcasted_iota(I32, (n_lat, slots), 0) == owner) & valid
     upper = one_hot(lax.broadcasted_iota(I32, (slots, slots), 0) < lanes((slots, slots)))
     before = dot(one_hot(owned), upper)
@@ -313,31 +282,11 @@
                 if levels > SMALL:
                     msg_out[2 * m + change, SMALL:levels, :] = full[SMALL:levels]
 
-    def msg_copy(n, change):
-        target = 2 * chip_at(n, 1) + lax.rem(core + change, 2)
-        return pltpu.make_async_remote_copy(
-            src_ref=msg_out.at[target],
-            dst_ref=msg_in.at[lat],
-            send_sem=msg_send.at[2 * n + change],
-            recv_sem=msg_recv.at[2 * n + change],
-            device_id={"lat": target},
-            device_id_type=MESH,
-        )
-
-    def others(n):
-        return (1,) if chips[n] == (0, 0) else (0, 1)
-
-
     group = max(1, len(chips) // 4)
     for g in range(0, len(chips), group):
         route([chip_at(n, 1) for n in range(g, g + group)])
-        for n in range(g, g + group):
-            for change in others(n):
-                msg_copy(n, change).start()
-    msg_in[lat] = msg_out[lat]
-
-
-    loads[6].wait()
+
+    loads[5].wait()
     for c in range(2):
         for p in range(TILES):
             a = cour_in[c, pl.ds(p, levels, stride=ROWS), :]
@@ -373,12 +322,58 @@
         return copies
 
     c_copies = edge_copies(c_lon_out, c_lon_in, c_lat_out, c_lat_in, c_send, c_recv)
+
+    def block(i):
+        return pl.ds(pl.multiple_of(i * 16, 16), 16)
+
+    def fwd_copy(t, d):
+        return pltpu.make_async_remote_copy(
+            src_ref=fwd_out.at[t, block(lev_at(d)), :],
+            dst_ref=fwd_in.at[t, block(lev), :],
+            send_sem=fwd_send.at[t, d],
+            recv_sem=fwd_recv.at[t, d],
+            device_id={"lev": lev_at(d)},
+            device_id_type=MESH,
+        )
+
+    def start_fwd(t):
+        def step(i, _):
+            fwd_copy(t, far(i)).start()
+            return _
+
+        lax.fori_loop(0, n_lev - 1, step, 0)
+
+    def msg_copy(n, change):
+        target = 2 * chip_at(n, 1) + lax.rem(core + change, 2)
+        return pltpu.make_async_remote_copy(
+            src_ref=msg_out.at[target],
+            dst_ref=msg_in.at[lat],
+            send_sem=msg_send.at[2 * n + change],
+            recv_sem=msg_recv.at[2 * n + change],
+            device_id={"lat": target},
+            device_id_type=MESH,
+        )
+
+    def others(n):
+        return (1,) if chips[n] == (0, 0) else (0, 1)
+
+
+    pl.semaphore_wait(barrier, n_lev + n_lat - 2)
+
+    start_fwd(0)
+    for n in range(len(chips)):
+        for change in others(n):
+            msg_copy(n, change).start()
+    start_fwd(1)
     for copy in c_copies:
         copy.start()
-
-
+    for t in range(2):
+        fwd_in[t, block(lev), :] = fwd_out[t, block(lev), :]
+    msg_in[lat] = msg_out[lat]
+
+
+    loads[6].wait()
     loads[7].wait()
-    loads[8].wait()
     for g in range(mat_in.shape[0] // 2):
         wide = []
         for odd in range(2):
@@ -412,10 +407,13 @@
         target = small_row(one, 3).astype(I32) - 1
         hot[:, at] = one_hot(lax.broadcasted_iota(I32, (columns, 128), 0) == target)
 
+
+    group = max(1, len(chips) // 2)
     for g in range(len(chips) // group):
         for n in range(g * group, (g + 1) * group):
             for change in others(n):
                 msg_copy(n, change).wait()
+        for n in range(g * group, (g + 1) * group):
             arrive(n)
         taken = pl.ds(g * group * 128, group * 128)
         for q in range(TILES // 2):
@@ -568,7 +566,7 @@
     for n in range(len(chips)):
         for change in others(n):
             ret_copy(n, change).start()
-    ret_in[lat] = ret_out[n_lat - 2 + core]
+    ret_in[lat] = ret_out[core]
     for n in range(len(chips)):
         for change in others(n):
             ret_copy(n, change).wait()
@@ -645,7 +643,7 @@
         sounding_count,
     )
     vm, dma = pltpu.VMEM, pltpu.SemaphoreType.DMA
-    scratch = [vm(x.shape, x.dtype) for x in operands]
+    scratch = [vm(x.shape, x.dtype) for x in operands[:-1]]
     scratch += [vm((2, n_lev * 16, 128), F32) for _ in range(3)]
     scratch += [vm((n_lat, levels, 128), F32) for _ in range(2)]
     scratch += [vm((n_lat, MSG, 128), F32) for _ in range(2)]
@@ -663,7 +661,7 @@
         vm((2, TILES, levels, 128), F32),
         vm((4 * levels, columns), BF16),
         vm((2 * MSG, spots), BF16),
-        dma((9,)),
+        dma((8,)),
         dma((2,)),
     ]
     scratch += [dma((2, n_lev)) for _ in range(4)]
@@ -678,7 +676,7 @@
             jax.ShapeDtypeStruct((2, n_lev * 16, 128), F32),
             jax.ShapeDtypeStruct((2, slots), F32),
         ),
-        in_specs=[in_hbm] * len(operands),
+        in_specs=[in_hbm] * (len(operands) - 1) + [pl.BlockSpec(memory_space=pltpu.SMEM)],
         out_specs=(in_hbm, in_vmem),
         scratch_shapes=scratch,
         compiler_params=pltpu.CompilerParams(

time: 54.1 us -> 51.4 us (0.950)
  Pallas kernels: 52.7 us -> 49.9 us
    pallas_call x1, Pallas kernels: 50.9 us -> 48.1 us  [per_device(): pl.pallas_call(functools.partial(kernel, n_lev, n_lat), out_shape=(jax.Sh...]
where the time goes in v5:
time: 51.4 us; the launch traced here: 51.2 us
  Pallas kernels  49.9 us (97%)
  between operations  1.29 us (3%)
    pallas_call x1, Pallas kernels, per_device(): pl.pallas_call(functools.partial(kernel, n_lev, n_lat), out_shape=(jax.Sh...  48.1 us
    pallas_call x1, Pallas kernels, per_device(): pl.pallas_call(functools.partial(finish, n_lev), out_shape=(jax.ShapeDtyp...  1.81 us

profile of v5, /device:TPU:1, one launch (start us, length us, event | category | flops | bytes accessed | tf_op | source)
XLA Modules:
  0.0 51.2 jit_solution(9110889777911845295)
XLA Ops:
  1.3 48.1 %shard_map.104 = (f32[2,256,128]{2,1,0:T(8,128)}, f32[2,512]{1,0:T(2,128)}) custom-call(f32[2,2,16,1024]{3,2,1,0:T(8,128)} %adj_hbm.1, f32[2,512,64]{2,1,0:T(8,128)} %bitcast.12, s32[16,64]{1,0:T(8,128)} %top_hbm.1, f32[16,32,32]{2,1,0:T(8,128)} %mat_hbm.1, f32[64,512]{1,0:T(8,128)} %bitcast.13, f32[2,512]{1,0:T(2,128)} %bitcast.14, s32[1,512]{1,0:T(1,128)} %bitcast.15, ...), custom_call_target="tpu_custom_call" | custom-call | tf_op jit(solution)/shard_map/pallas_call | solution.py:673
  49.4 1.8 %shard_map.105 = (f32[2,2,16,1024]{3,2,1,0:T(8,128)}, f32[2,512]{1,0:T(2,128)}) custom-call(f32[2,256,128]{2,1,0:T(8,128)} %get-tuple-element.6.back_hbm, f32[2,512]{1,0:T(2,128)} %get-tuple-element.7.sens_hbm), custom_call_target="tpu_custom_call" | custom-call | tf_op jit(solution)/shard_map/pallas_call | solution.py:686

commit v6 on v5

--- a/solution.py
+++ b/solution.py
@@ -57,7 +57,19 @@
         here = x // 2 == p
         to_west = jnp.where(here, turn(tiles[p], 2 * p), to_west)
         to_east = jnp.where(here, turn(tiles[p], 2 * p + 66), to_east)
-    return to_west, to_east
+    return tuple(fold(edge) for edge in (to_west, to_east))
+
+
+def fold(edge):
+    out = edge[0:8]
+    for i in range(1, edge.shape[0] // 8):
+        here = lanes(out.shape) % HALF // 16 == i
+        out = jnp.where(here, turn(edge[8 * i : 8 * i + 8], 16 * i), out)
+    return out
+
+
+def unfold(edge, levels):
+    return jnp.concatenate([turn(edge, -16 * i) for i in range(levels // 8)], axis=0)
 
 
 def shift_lon(tile, p, from_west, from_east, steps):
@@ -122,7 +134,7 @@
     cell_hbm,
     count_ref,
     back_in,
-    sens_ref,
+    sens_out,
     adj_in,
     cour_in,
     top_in,
@@ -157,6 +169,7 @@
     conv,
     conv_split,
     ret_split,
+    sens,
     in_sem,
     keep_sem,
     fwd_send,
@@ -197,7 +210,7 @@
 
     def far(i):
         half = (i + 1) // 2
-        return n_lev // 2 + half * (1 - 2 * lax.rem(i, 2))
+        return n_lev // 2 + half * (1 - 2 * (i % 2))
 
     loads = [
         pltpu.make_async_copy(source, target, in_sem.at[i])
@@ -428,11 +441,8 @@
 
 
     def wait_fwd(t):
-        def step(d, _):
-            fwd_copy(t, d).wait()
-            return _
-
-        lax.fori_loop(1, n_lev, step, 0)
+        for i in range(n_lev - 1):
+            fwd_copy(t, far(i)).wait()
 
     a_copies = []
     for t in range(2):
@@ -478,7 +488,7 @@
     first, last = lat == 0, lat == n_lat - 1
     for copy in c_copies:
         copy.wait()
-    from_east, from_west = c_lon_in[0], c_lon_in[1]
+    from_east, from_west = unfold(c_lon_in[0], levels), unfold(c_lon_in[1], levels)
     from_north, from_south = c_lat_in[0], c_lat_in[1]
     from_north = jnp.where(last, 0.0, from_north)
     from_south = jnp.where(first, 0.0, from_south)
@@ -510,7 +520,7 @@
     for t in range(2):
         for copy in a_copies[t]:
             copy.wait()
-        from_east, from_west = a_lon_in[t, 0], a_lon_in[t, 1]
+        from_east, from_west = (unfold(a_lon_in[t, i], levels) for i in range(2))
         from_north, from_south = a_lat_in[t, 0], a_lat_in[t, 1]
         from_north = jnp.where(last, 0.0, from_north)
         from_south = jnp.where(first, 0.0, from_south)
@@ -576,17 +586,16 @@
         ret_split[:, pl.ds(m * 128, 128)] = jnp.concatenate(split(both), axis=0)
     own = dot(ret_split[...], place[...])
     own = own[:MSG] + own[MSG:]
-    sens_ref[...] = own[0:2]
+    sens[...] = own[0:2]
+    sens_store = pltpu.make_async_copy(sens, sens_out, keep_sem.at[2])
+    sens_store.start()
 
 
     for t in range(2):
-
-        def wait_back(d, _, t=t):
-            back_copy(t, d).wait()
-            return _
-
-        lax.fori_loop(1, n_lev, wait_back, 0)
+        for i in range(n_lev - 1):
+            back_copy(t, far(i)).wait()
         keeps[t].wait()
+    sens_store.wait()
 
 
 def finish(n_lev, back_hbm, sens_hbm, out_hbm, sens_out, back, out, load_sem, store_sem):
@@ -647,8 +656,10 @@
     scratch += [vm((2, n_lev * 16, 128), F32) for _ in range(3)]
     scratch += [vm((n_lat, levels, 128), F32) for _ in range(2)]
     scratch += [vm((n_lat, MSG, 128), F32) for _ in range(2)]
-    scratch += [vm((2, levels, 128), F32) for _ in range(4)]
-    scratch += [vm((2, 2, levels, 128), F32) for _ in range(4)]
+    scratch += [vm((2, 8, 128), F32) for _ in range(2)]
+    scratch += [vm((2, levels, 128), F32) for _ in range(2)]
+    scratch += [vm((2, 2, 8, 128), F32) for _ in range(2)]
+    scratch += [vm((2, 2, levels, 128), F32) for _ in range(2)]
     scratch += [
         vm((spots, slots), BF16),
         vm((n_lat // 2, 2 * levels, 128), F32),
@@ -661,15 +672,15 @@
         vm((2, TILES, levels, 128), F32),
         vm((4 * levels, columns), BF16),
         vm((2 * MSG, spots), BF16),
+        vm((2, slots), F32),
         dma((8,)),
-        dma((2,)),
+        dma((3,)),
     ]
     scratch += [dma((2, n_lev)) for _ in range(4)]
     scratch += [dma((n_lat,)) for _ in range(4)]
     scratch += [dma((4,)) for _ in range(2)]
     scratch += [dma((2, 4)) for _ in range(2)]
     in_hbm = pl.BlockSpec(memory_space=pltpu.HBM)
-    in_vmem = pl.BlockSpec(memory_space=pltpu.VMEM)
     back, sens = pl.pallas_call(
         functools.partial(kernel, n_lev, n_lat),
         out_shape=(
@@ -677,7 +688,7 @@
             jax.ShapeDtypeStruct((2, slots), F32),
         ),
         in_specs=[in_hbm] * (len(operands) - 1) + [pl.BlockSpec(memory_space=pltpu.SMEM)],
-        out_specs=(in_hbm, in_vmem),
+        out_specs=(in_hbm, in_hbm),
         scratch_shapes=scratch,
         compiler_params=pltpu.CompilerParams(
             collective_id=0, has_side_effects=True, vmem_limit_bytes=60 * 2**20

time: 51.4 us -> 50.7 us (0.986)
  Pallas kernels: 49.9 us -> 49.2 us
    pallas_call x1, Pallas kernels: 48.1 us -> 47.4 us  [per_device(): pl.pallas_call(functools.partial(kernel, n_lev, n_lat), out_shape=(jax.Sh...]
where the time goes in v6:
time: 50.7 us; the launch traced here: 50.5 us
  Pallas kernels  49.2 us (97%)
  between operations  1.29 us (3%)
    pallas_call x1, Pallas kernels, per_device(): pl.pallas_call(functools.partial(kernel, n_lev, n_lat), out_shape=(jax.Sh...  47.4 us
    pallas_call x1, Pallas kernels, per_device(): pl.pallas_call(functools.partial(finish, n_lev), out_shape=(jax.ShapeDtyp...  1.81 us

profile of v6, /device:TPU:1, one launch (start us, length us, event | category | flops | bytes accessed | tf_op | source)
XLA Modules:
  0.0 50.5 jit_solution(8829668160711404809)
XLA Ops:
  1.3 47.4 %shard_map.104 = (f32[2,256,128]{2,1,0:T(8,128)}, f32[2,512]{1,0:T(2,128)}) custom-call(f32[2,2,16,1024]{3,2,1,0:T(8,128)} %adj_hbm.1, f32[2,512,64]{2,1,0:T(8,128)} %bitcast.12, s32[16,64]{1,0:T(8,128)} %top_hbm.1, f32[16,32,32]{2,1,0:T(8,128)} %mat_hbm.1, f32[64,512]{1,0:T(8,128)} %bitcast.13, f32[2,512]{1,0:T(2,128)} %bitcast.14, s32[1,512]{1,0:T(1,128)} %bitcast.15, ...), custom_call_target="tpu_custom_call" | custom-call | tf_op jit(solution)/shard_map/pallas_call | solution.py:684
  48.7 1.8 %shard_map.105 = (f32[2,2,16,1024]{3,2,1,0:T(8,128)}, f32[2,512]{1,0:T(2,128)}) custom-call(f32[2,256,128]{2,1,0:T(8,128)} %get-tuple-element.6.back_hbm, f32[2,512]{1,0:T(2,128)} %get-tuple-element.7.sens_hbm), custom_call_target="tpu_custom_call" | custom-call | tf_op jit(solution)/shard_map/pallas_call | solution.py:697

commit v7 on v6

--- a/solution.py
+++ b/solution.py
@@ -15,6 +15,7 @@
 USED = 48
 SMALL = 8
 MSG = 8
+CHUNKS = 2
 
 
 def lanes(shape):
@@ -599,16 +600,31 @@
 
 
 def finish(n_lev, back_hbm, sens_hbm, out_hbm, sens_out, back, out, load_sem, store_sem):
+    pairs = n_lev // 2
+    wide = max(1, pairs // CHUNKS)
+    sens_copy = pltpu.make_async_copy(sens_hbm, sens_out, store_sem.at[2 * CHUNKS])
     loads, stores = [], []
     for t in range(2):
-        loads.append(pltpu.make_async_copy(back_hbm.at[t], back.at[t], load_sem.at[t]))
-        loads[t].start()
-        stores.append(pltpu.make_async_copy(out.at[t], out_hbm.at[t], store_sem.at[t]))
-    sens_copy = pltpu.make_async_copy(sens_hbm, sens_out, store_sem.at[2])
+        for c in range(pairs // wide):
+            rows, cols = pl.ds(c * wide * 32, wide * 32), pl.ds(c * wide * 128, wide * 128)
+            i = t * CHUNKS + c
+            loads.append(
+                pltpu.make_async_copy(
+                    back_hbm.at[t, rows, :], back.at[t, rows, :], load_sem.at[i]
+                )
+            )
+            stores.append(
+                pltpu.make_async_copy(
+                    out.at[t, :, :, cols], out_hbm.at[t, :, :, cols], store_sem.at[i]
+                )
+            )
+    for load in loads:
+        load.start()
     sens_copy.start()
-    for t in range(2):
-        loads[t].wait()
-        for m in range(n_lev // 2):
+    for i, (load, store) in enumerate(zip(loads, stores)):
+        t, c = i // (pairs // wide), i % (pairs // wide)
+        load.wait()
+        for m in range(c * wide, (c + 1) * wide):
             for kk in range(2):
                 a, b = pair(
                     back[t, pl.ds(m * 32 + kk * 8, 8), :],
@@ -616,7 +632,7 @@
                 )
                 out[t, kk, 0:8, pl.ds(m * 128, 128)] = a
                 out[t, kk, 8:16, pl.ds(m * 128, 128)] = b
-        stores[t].start()
+        store.start()
     for store in stores:
         store.wait()
     sens_copy.wait()
@@ -705,8 +721,8 @@
         scratch_shapes=[
             vm((2, n_lev * 16, 128), F32),
             vm(adjoint_in.shape, F32),
-            dma((2,)),
-            dma((3,)),
+            dma((2 * CHUNKS,)),
+            dma((2 * CHUNKS + 1,)),
         ],
         compiler_params=pltpu.CompilerParams(vmem_limit_bytes=60 * 2**20),
     )(back, sens)

time: 50.7 us -> 50.8 us (level)
  no operation moved by 1% of the time
where the time goes in v7:
time: 50.8 us; the launch traced here: 50.6 us
  Pallas kernels  49.3 us (97%)
  between operations  1.29 us (3%)
    pallas_call x1, Pallas kernels, per_device(): pl.pallas_call(functools.partial(kernel, n_lev, n_lat), out_shape=(jax.Sh...  47.4 us
    pallas_call x1, Pallas kernels, per_device(): pl.pallas_call(functools.partial(finish, n_lev), out_shape=(jax.ShapeDtyp...  1.89 us

profile of v7, /device:TPU:1, one launch (start us, length us, event | category | flops | bytes accessed | tf_op | source)
XLA Modules:
  0.0 50.6 jit_solution(12145736337414860592)
XLA Ops:
  1.3 47.4 %shard_map.104 = (f32[2,256,128]{2,1,0:T(8,128)}, f32[2,512]{1,0:T(2,128)}) custom-call(f32[2,2,16,1024]{3,2,1,0:T(8,128)} %adj_hbm.1, f32[2,512,64]{2,1,0:T(8,128)} %bitcast.12, s32[16,64]{1,0:T(8,128)} %top_hbm.1, f32[16,32,32]{2,1,0:T(8,128)} %mat_hbm.1, f32[64,512]{1,0:T(8,128)} %bitcast.13, f32[2,512]{1,0:T(2,128)} %bitcast.14, s32[1,512]{1,0:T(1,128)} %bitcast.15, ...), custom_call_target="tpu_custom_call" | custom-call | tf_op jit(solution)/shard_map/pallas_call | solution.py:700
  48.7 1.9 %shard_map.105 = (f32[2,2,16,1024]{3,2,1,0:T(8,128)}, f32[2,512]{1,0:T(2,128)}) custom-call(f32[2,256,128]{2,1,0:T(8,128)} %get-tuple-element.6.back_hbm, f32[2,512]{1,0:T(2,128)} %get-tuple-element.7.sens_hbm), custom_call_target="tpu_custom_call" | custom-call | tf_op jit(solution)/shard_map/pallas_call | solution.py:713
